TPU v7x, 512 devices: a whole 4x8x8 slice. The times are simulated.
512 devices in a mesh: ep: 128 (over z, y, core), dp: 4 (over x).
Axes of the slice: x: 4, y: 8, z: 8, core: 2. Of those that a mesh axis runs over, the one named last changes fastest.
Arguments:
- tokens: bfloat16 [65536, 2048], P(('dp', 'ep')), parts along dimension 0, may hold values from -6 to 6
- expert_ids: int32 [65536, 4], P(('dp', 'ep')), parts along dimension 0, may hold values from 0 to 127, all different within a row; in each aligned block of 128 rows (0 to 127, 128 to 255, ...) at most 6 rows name the same one
- gate_values: float32 [65536, 4], P(('dp', 'ep')), parts along dimension 0, may hold values from 0.1 to 1
- latent_down: bfloat16 [2048, 512], P('ep'), may hold values from -0.125 to 0.125
- latent_up: bfloat16 [512, 2048], P(None, 'ep'), may hold values from -0.25 to 0.25
- expert_up: bfloat16 [128, 512, 1408], P('ep'), may hold values from -0.25 to 0.25
- expert_down: bfloat16 [128, 1408, 512], P('ep'), may hold values from -0.15625 to 0.15625
- grad_out: bfloat16 [65536, 2048], P(('dp', 'ep')), parts along dimension 0, may hold values from -6 to 6
Outputs:
- layer_out: bfloat16 [65536, 2048], P(('dp', 'ep')), parts along dimension 0
- grad_tokens: bfloat16 [65536, 2048], P(('dp', 'ep')), parts along dimension 0
There are 4 independent parts, one for each index of `dp`. A program takes and returns all parts, laid end to end along the dimension named above; an argument that names none is the same for every part. Nothing has to cross between parts.
Inputs may be any that keep to these rules, and one draw needn't show every extreme that they name: `expert_ids`: each row names 4 different experts. Among the 128 tokens of one device, no expert is named by more than 6 tokens, and in every draw some expert is named by exactly 6 tokens of some device.
All inputs are finite; a program needn't handle non-finite values.
Results may differ from a plain program's by a relative error of at most 0.013.
Values may be sent and summed in bfloat16 or wider, within the bound.
No kernel may reach another device: no remote copies, remote signals or barrier semaphores. Data moves between devices by JAX's collectives and lax.ppermute only.
A program may use at most 64 MiB of HBM per device.

v0:
```python
import jax
import jax.numpy as jnp
from jax import lax
from jax.sharding import PartitionSpec as P


def contract_last(left, right):
    return lax.dot_general(
        left, right, (((1,), (1,)), ((), ())), preferred_element_type=jnp.float32
    )


def on_device(
    tokens, expert_ids, gate_values, latent_down, latent_up, expert_up, expert_down, grad_out
):
    ep_size = lax.axis_size("ep")
    tok_rows = expert_ids.shape[0]
    top_count = expert_ids.shape[1]
    local_experts = expert_up.shape[0]
    width = latent_up.shape[0]
    experts = local_experts * ep_size
    capacity = max(2, (3 * tok_rows * top_count + 2 * experts - 1) // (2 * experts))
    full_down, full_up = (
        lax.all_gather(latent_down, "ep", axis=0, tiled=True),
        lax.all_gather(latent_up, "ep", axis=1, tiled=True),
    )
    latent = jnp.dot(tokens, full_down, preferred_element_type=jnp.float32).astype(jnp.bfloat16)
    numbers = jnp.arange(experts, dtype=jnp.int32)
    picked = (expert_ids[:, :, None] == numbers[None, None, :]).astype(jnp.int32)
    routed = jnp.sum(picked, axis=1)
    before = jnp.cumsum(routed, axis=0) - routed
    slot_pos = jnp.sum(picked * before[:, None, :], axis=2)
    flat_slot = expert_ids * capacity + slot_pos
    positions = jnp.arange(experts * capacity, dtype=jnp.int32)
    matches = flat_slot[None, :, :] == positions[:, None, None]
    placing = jnp.any(matches, axis=2).astype(jnp.bfloat16)
    gate_place = jnp.sum(jnp.where(matches, gate_values[None, :, :], 0.0), axis=2)
    outbound = jnp.dot(placing, latent, preferred_element_type=jnp.float32).astype(jnp.bfloat16)
    outbound = outbound.reshape(ep_size, local_experts, capacity, width)
    pre_act = jnp.einsum(
        "sjml,jlf->sjmf",
        lax.all_to_all(outbound, "ep", split_axis=0, concat_axis=0, tiled=True),
        expert_up,
        preferred_element_type=jnp.float32,
    )
    squared = jnp.square(jax.nn.relu(pre_act)).astype(jnp.bfloat16)
    expert_out = jnp.einsum(
        "sjmf,jfl->sjml", squared, expert_down, preferred_element_type=jnp.float32
    ).astype(jnp.bfloat16)
    expert_out, stored = (expert_out, pre_act)
    returned = lax.all_to_all(expert_out, "ep", split_axis=0, concat_axis=0, tiled=True).reshape(
        experts * capacity, width
    )
    gathered_rows = jnp.take(returned, flat_slot, axis=0)
    combined = jnp.sum(gate_values[:, :, None] * gathered_rows.astype(jnp.float32), axis=1).astype(
        jnp.bfloat16
    )
    layer_full = jnp.dot(combined, full_up, preferred_element_type=jnp.float32)
    grad_latent = contract_last(grad_out, full_up)
    layer_out = layer_full.astype(jnp.bfloat16)
    grad_send = jnp.dot(
        gate_place, grad_latent, precision=lax.Precision.HIGHEST, preferred_element_type=jnp.float32
    )
    grad_send = grad_send.astype(jnp.bfloat16).reshape(ep_size, local_experts, capacity, width)
    grad_arrived = lax.all_to_all(grad_send, "ep", split_axis=0, concat_axis=0, tiled=True)
    pre_act = stored
    grad_act = jnp.einsum(
        "sjml,jfl->sjmf", grad_arrived, expert_down, preferred_element_type=jnp.float32
    )
    grad_pre = (2.0 * jax.nn.relu(pre_act) * grad_act).astype(jnp.bfloat16)
    grad_in = jnp.einsum(
        "sjmf,jlf->sjml", grad_pre, expert_up, preferred_element_type=jnp.float32
    ).astype(jnp.bfloat16)
    grad_back = lax.all_to_all(grad_in, "ep", split_axis=0, concat_axis=0, tiled=True).reshape(
        experts * capacity, width
    )
    grad_sum = jnp.sum(jnp.take(grad_back, flat_slot, axis=0).astype(jnp.float32), axis=1).astype(
        jnp.bfloat16
    )
    grad_tokens = contract_last(grad_sum, full_down).astype(jnp.bfloat16)
    return (layer_out, grad_tokens)


def solution(mesh):
    placed = (
        P(("dp", "ep"), None),
        P(("dp", "ep"), None),
        P(("dp", "ep"), None),
        P("ep", None),
        P(None, "ep"),
        P("ep", None, None),
        P("ep", None, None),
        P(("dp", "ep"), None),
    )
    return jax.shard_map(
        on_device,
        mesh=mesh,
        in_specs=placed,
        out_specs=(P(("dp", "ep"), None), P(("dp", "ep"), None)),
        check_vma=False,
    )
```

profile of v0, /device:TPU:1, one launch (start us, length us, event | category | flops | bytes accessed | tf_op | source)
XLA Modules:
  0.0 342.6 jit_solution(10094555136022475105)
XLA Ops:
  12.0 87.9 %all-gather.3.cloned.1.call-done = bf16[2048,512]{1,0:T(8,128)(2,1)} async-done(((bf16[16,512]{1,0:T(8,128)(2,1)}), bf16[2048,512]{1,0:T(8,128)(2,1)}) %all-gather.3.cloned.1.call-update) | async-done | bytes 2097168 | tf_op jit(solution)/shard_map/all_gather | solution.py:24
  99.9 2.6 convolution_convert_fusion.3
  103.8 9.5 %all-to-all-start = ((bf16[128,1,6,512]{3,2,1,0:T(8,128)(2,1)}), bf16[128,1,6,512]{3,2,1,0:T(8,128)(2,1)S(1)}, u32[]{:S(2)}, u32[]{:S(2)}) async-start(bf16[128,1,6,512]{3,2,1,0:T(8,128)(2,1)} %bitcast), calls=%async_computation | async-start | bytes 2097152 | tf_op jit(solution)/shard_map/all_to_all | solution.py:42
  114.2 81.3 %all-gather.5.cloned.1.call-done = bf16[512,2048]{0,1:T(8,128)(2,1)} async-done(((bf16[512,16]{0,1:T(8,128)(2,1)}), bf16[512,2048]{0,1:T(8,128)(2,1)}) %all-gather.5.cloned.1.call-update) | async-done | bytes 2097168 | tf_op jit(solution)/shard_map/all_gather | solution.py:25
  195.5 2.1 fusion.33
  197.6 1.4 convolution_convert_fusion.2
  200.3 9.5 %all-to-all-start.2 = ((bf16[128,1,6,512]{3,2,1,0:T(8,128)(2,1)}), bf16[128,1,6,512]{3,2,1,0:T(8,128)(2,1)S(1)}, u32[]{:S(2)}, u32[]{:S(2)}) async-start(bf16[128,1,6,512]{3,2,1,0:T(8,128)(2,1)} %bitcast.9), calls=%async_computation.2 | async-start | bytes 2097152 | tf_op jit(solution)/shard_map/all_to_all | solution.py:65
  209.9 3.4 fusion.7
  213.3 27.5 %all-to-all-done.2 = bf16[128,1,6,512]{3,2,1,0:T(8,128)(2,1)S(1)} async-done(((bf16[128,1,6,512]{3,2,1,0:T(8,128)(2,1)}), bf16[128,1,6,512]{3,2,1,0:T(8,128)(2,1)S(1)}, u32[]{:S(2)}, u32[]{:S(2)}) %all-to-all-start.2) | async-done | bytes 786464 | tf_op jit(solution)/shard_map/all_to_all | solution.py:65
  240.8 5.4 %fusion.18 = bf16[128,1,6,512]{3,0,2,1:T(8,128)(2,1)S(1)} fusion(bf16[1,512,1408]{2,1,0:T(8,128)(2,1)S(1)} %copy-done, f32[128,6,1408]{2,0,1:T(8,128)} %fusion.7, bf16[1,1408,512]{2,1,0:T(8,128)(2,1)} %param.16, bf16[128,1,6,512]{3,2,1,0:T(8,128)(2,1)S(1)} %all-to-all-done.2), kind=kOutput, calls=%fused_computation.22 | convolution fusion | flops 2219311104 | bytes 8781824 | tf_op jit(solution)/shard_map/sjmf,jlf->sjml/dot_general | solution.py:71
  246.2 1.5 copy.51
  247.7 6.5 %all-to-all-start.3 = ((bf16[128,1,6,512]{3,2,1,0:T(8,128)(2,1)}), bf16[128,1,6,512]{3,2,1,0:T(8,128)(2,1)S(1)}, u32[]{:S(2)}, u32[]{:S(2)}) async-start(bf16[128,1,6,512]{3,2,1,0:T(8,128)(2,1)} %copy.51), calls=%async_computation.3 | async-start | bytes 2097152 | tf_op jit(solution)/shard_map/all_to_all | solution.py:74
  254.2 4.0 %fusion.15 = bf16[128,1,6,512]{3,0,2,1:T(8,128)(2,1)S(1)} fusion(bf16[1,1408,512]{2,1,0:T(8,128)(2,1)} %param.16, f32[128,6,1408]{2,0,1:T(8,128)} %fusion.7), kind=kOutput, calls=%fused_computation.21 | convolution fusion | flops 1110933504 | bytes 6553600 | tf_op jit(solution)/shard_map/sjmf,jfl->sjml/dot_general | solution.py:47
  258.3 1.4 copy.46
  259.7 25.4 %all-to-all-done.3 = bf16[128,1,6,512]{3,2,1,0:T(8,128)(2,1)S(1)} async-done(((bf16[128,1,6,512]{3,2,1,0:T(8,128)(2,1)}), bf16[128,1,6,512]{3,2,1,0:T(8,128)(2,1)S(1)}, u32[]{:S(2)}, u32[]{:S(2)}) %all-to-all-start.3) | async-done | bytes 786464 | tf_op jit(solution)/shard_map/all_to_all | solution.py:74
  285.1 6.9 %all-to-all-start.1 = ((bf16[128,1,6,512]{3,2,1,0:T(8,128)(2,1)}), bf16[128,1,6,512]{3,2,1,0:T(8,128)(2,1)}, u32[]{:S(2)}, u32[]{:S(2)}) async-start(bf16[128,1,6,512]{3,2,1,0:T(8,128)(2,1)} %copy.46), calls=%async_computation.1 | async-start | bytes 2097152 | tf_op jit(solution)/shard_map/all_to_all | solution.py:51
  293.4 2.0 gather_fusion.1
  296.3 26.3 %all-to-all-done.1 = bf16[128,1,6,512]{3,2,1,0:T(8,128)(2,1)} async-done(((bf16[128,1,6,512]{3,2,1,0:T(8,128)(2,1)}), bf16[128,1,6,512]{3,2,1,0:T(8,128)(2,1)}, u32[]{:S(2)}, u32[]{:S(2)}) %all-to-all-start.1) | async-done | bytes 786464 | tf_op jit(solution)/shard_map/all_to_all | solution.py:51
  324.0 2.6 gather_fusion
  326.6 2.1 reshape.98
  328.7 1.8 select_reduce_fusion.1
  330.6 1.9 multiply_reduce_fusion
  332.5 1.6 convolution_convert_fusion
  334.1 1.6 convolution_convert_fusion.1
  (37 shorter events, 12.0 us)
Async XLA Ops:
  7.2 202.7 %copy-start = (bf16[1,512,1408]{2,1,0:T(8,128)(2,1)S(1)}, bf16[1,512,1408]{2,1,0:T(8,128)(2,1)}, u32[]{:S(2)}) copy-start(bf16[1,512,1408]{2,1,0:T(8,128)(2,1)} %param.15) | copy-start | bytes 4325380
  7.2 92.8 %all-gather.3.cloned.1.call-start = ((), (), s32[]{:S(2)}) async-start(), calls=%async_computation.4 | async-start | bytes 2113536 | tf_op jit(solution)/shard_map/all_gather | solution.py:24
  7.9 187.6 %all-gather.5.cloned.1.call-start = ((), (), s32[]{:S(2)}) async-start(), calls=%async_computation.5 | async-start | bytes 2113536 | tf_op jit(solution)/shard_map/all_gather | solution.py:25
  102.5 10.8 %copy-start.5 = (f32[128,4]{0,1:T(4,128)S(1)}, f32[128,4]{0,1:T(4,128)}, u32[]{:S(2)}) copy-start(f32[128,4]{0,1:T(4,128)} %param.12) | copy-start | bytes 6148
  102.5 93.0 %copy-start.4 = (bf16[128,2048]{1,0:T(8,128)(2,1)S(1)}, bf16[128,2048]{1,0:T(8,128)(2,1)}, u32[]{:S(2)}) copy-start(bf16[128,2048]{1,0:T(8,128)(2,1)} %param.17) | copy-start | bytes 1572868
  103.8 96.6 %all-to-all-start = ((bf16[128,1,6,512]{3,2,1,0:T(8,128)(2,1)}), bf16[128,1,6,512]{3,2,1,0:T(8,128)(2,1)S(1)}, u32[]{:S(2)}, u32[]{:S(2)}) async-start(bf16[128,1,6,512]{3,2,1,0:T(8,128)(2,1)} %bitcast), calls=%async_computation | async-start | bytes 2097152 | tf_op jit(solution)/shard_map/all_to_all | solution.py:42
  195.5 2.1 copy-start.3
  200.3 40.4 %all-to-all-start.2 = ((bf16[128,1,6,512]{3,2,1,0:T(8,128)(2,1)}), bf16[128,1,6,512]{3,2,1,0:T(8,128)(2,1)S(1)}, u32[]{:S(2)}, u32[]{:S(2)}) async-start(bf16[128,1,6,512]{3,2,1,0:T(8,128)(2,1)} %bitcast.9), calls=%async_computation.2 | async-start | bytes 2097152 | tf_op jit(solution)/shard_map/all_to_all | solution.py:65
  247.7 37.4 %all-to-all-start.3 = ((bf16[128,1,6,512]{3,2,1,0:T(8,128)(2,1)}), bf16[128,1,6,512]{3,2,1,0:T(8,128)(2,1)S(1)}, u32[]{:S(2)}, u32[]{:S(2)}) async-start(bf16[128,1,6,512]{3,2,1,0:T(8,128)(2,1)} %copy.51), calls=%async_computation.3 | async-start | bytes 2097152 | tf_op jit(solution)/shard_map/all_to_all | solution.py:74
  258.2 34.7 %copy-start.6 = (pred[128,4]{0,1:T(4,128)(4,1)S(1)}, pred[128,4]{0,1:T(4,128)(4,1)}, u32[]{:S(2)}) copy-start(pred[128,4]{0,1:T(4,128)(4,1)} %get-tuple-element.3) | copy-start | bytes 1540
  285.1 37.5 %all-to-all-start.1 = ((bf16[128,1,6,512]{3,2,1,0:T(8,128)(2,1)}), bf16[128,1,6,512]{3,2,1,0:T(8,128)(2,1)}, u32[]{:S(2)}, u32[]{:S(2)}) async-start(bf16[128,1,6,512]{3,2,1,0:T(8,128)(2,1)} %copy.46), calls=%async_computation.1 | async-start | bytes 2097152 | tf_op jit(solution)/shard_map/all_to_all | solution.py:51
  326.6 5.9 %copy-start.1 = (bf16[2048,512]{1,0:T(8,128)(2,1)S(1)}, bf16[2048,512]{1,0:T(8,128)(2,1)}, u32[]{:S(2)}) copy-start(bf16[2048,512]{1,0:T(8,128)(2,1)} %all-gather.3.cloned.1.call-done) | copy-start | bytes 6291460
  328.7 5.4 %copy-start.2 = (bf16[512,2048]{0,1:T(8,128)(2,1)S(1)}, bf16[512,2048]{0,1:T(8,128)(2,1)}, u32[]{:S(2)}) copy-start(bf16[512,2048]{0,1:T(8,128)(2,1)} %all-gather.5.cloned.1.call-done) | copy-start | bytes 6291460
Sparse Core Ops, SparseCore 0:
  11.1 88.7 all-gather.2
  103.1 92.4 all-gather.4
where the time goes:
time: 343 us
  waiting for transfers between devices  250 us (73%)
  starting transfers between devices  32.5 us (9%)
  matrix products  22.1 us (6%)
  local copies, waits for them, and re-layouts  15.9 us (5%)
  between operations  14.2 us (4%)
  other arithmetic  8.04 us (2%)
    all_gather x1, waiting for transfers between devices, on_device(): lax.all_gather(latent_down, 'ep', axis=0, tiled=True)  87.9 us
    all_gather x1, waiting for transfers between devices, on_device(): lax.all_gather(latent_up, 'ep', axis=1, tiled=True)  81.3 us
    all_to_all x1, waiting for transfers between devices, on_device(): lax.all_to_all(grad_send, 'ep', split_axis=0, concat_axis=0, tiled=True)  27.5 us
    all_to_all x1, waiting for transfers between devices, on_device(): lax.all_to_all(expert_out, 'ep', split_axis=0, concat_axis=0, tiled=True)  26.3 us
    all_to_all x1, waiting for transfers between devices, on_device(): lax.all_to_all(grad_in, 'ep', split_axis=0, concat_axis=0, tiled=True)  25.4 us
    all_to_all x1, starting transfers between devices, on_device(): lax.all_to_all(outbound, 'ep', split_axis=0, concat_axis=0, tiled=True)  9.51 us
    all_to_all x1, starting transfers between devices, on_device(): lax.all_to_all(grad_send, 'ep', split_axis=0, concat_axis=0, tiled=True)  9.5 us
    all_to_all x1, starting transfers between devices, on_device(): lax.all_to_all(expert_out, 'ep', split_axis=0, concat_axis=0, tiled=True)  6.94 us
  transfers between devices with their start and end apart: 6, of which 5 were waited for; matrix products, arithmetic and copies ran while one was open for 8% of the time, Pallas kernels for 0%

commit v1 on v0

v1 whole, which is shorter than its diff:
```python
import functools

import jax
import jax.numpy as jnp
from jax import lax
from jax.experimental import pallas as pl
from jax.experimental.pallas import tpu as pltpu
from jax.sharding import PartitionSpec as P

SLOTS = 6
LANES = 128
MIB = 2**20


def dot(left, right):
    return jnp.dot(left, right, preferred_element_type=jnp.float32)


def contract_last(left, right):
    return lax.dot_general(
        left, right, (((1,), (1,)), ((), ())), preferred_element_type=jnp.float32
    )


def vmem_call(body, out_shape, scratch, limit_mib, flops, moved):
    return pl.pallas_call(
        body,
        out_shape=out_shape,
        scratch_shapes=scratch,
        compiler_params=pltpu.CompilerParams(vmem_limit_bytes=limit_mib * MIB),
        cost_estimate=pl.CostEstimate(flops=flops, bytes_accessed=moved, transcendentals=0),
    )


def route_kernel(experts, own_ids, other_ids, gates, place_ref, high_ref, low_ref):
    tok = own_ids.shape[1]
    number = lax.broadcasted_iota(jnp.int32, (experts, tok), 0)
    earlier = (
        lax.broadcasted_iota(jnp.int32, (tok, tok), 0)
        < lax.broadcasted_iota(jnp.int32, (tok, tok), 1)
    ).astype(jnp.bfloat16)
    for half, ids in enumerate((own_ids, other_ids)):
        routed = jnp.zeros((experts, tok), jnp.float32)
        weight = jnp.zeros((experts, tok), jnp.float32)
        for k in range(ids.shape[0]):
            named = ids[k : k + 1, :] == number
            routed += jnp.where(named, 1.0, 0.0)
            if half == 0:
                weight += jnp.where(named, gates[k : k + 1, :], 0.0)
        before = dot(routed.astype(jnp.bfloat16), earlier)
        for s in range(SLOTS):
            here = before == float(s)
            place_ref[half * SLOTS + s] = jnp.where(here, routed, 0.0).astype(jnp.bfloat16)
            if half == 0:
                gate = jnp.transpose(jnp.where(here, weight, 0.0))
                high = gate.astype(jnp.bfloat16)
                at = pl.ds(s * experts, experts)
                high_ref[:, at] = high
                low_ref[:, at] = (gate - high.astype(jnp.float32)).astype(jnp.bfloat16)


def whole_weight(w_ref):
    shards, rows, lanes = w_ref.shape
    per = 16
    parts = [
        w_ref[:, j * per : (j + 1) * per, :].reshape(shards * per, lanes)
        for j in range(rows // per)
    ]
    return jnp.concatenate(parts, axis=1)


def send_kernel(experts, own_ref, other_ref, w_ref, place_ref, out_ref, scr):
    tok = own_ref.shape[0]
    weight = whole_weight(w_ref)
    block = out_ref.shape[0] // experts
    for half, x_ref in enumerate((own_ref, other_ref)):
        latent = dot(x_ref[...], weight).astype(jnp.bfloat16)
        for s in range(SLOTS):
            rows = dot(place_ref[half * SLOTS + s], latent)
            for j in range(rows.shape[1] // LANES):
                first = (half * SLOTS + s) * (rows.shape[1] // LANES) + j
                scr[pl.ds(first, experts, stride=block), :] = rows[:, j * LANES : (j + 1) * LANES]
    out_ref[...] = scr[...].astype(jnp.bfloat16)


def expert_kernel(chips, in_ref, up_ref, down_ref, out_ref, scr, lat, grad):
    width = lat.shape[1]
    chunks = width // LANES
    block = 2 * SLOTS * chunks
    scr[...] = in_ref[...].astype(jnp.float32)
    for core in range(2):
        for s in range(SLOTS):
            slot = core * SLOTS + s
            for j in range(chunks):
                at = (pl.ds(slot * chips, chips), pl.ds(j * LANES, LANES))
                first = (core * SLOTS + s) * chunks + j
                lat[at] = scr[pl.ds(first, chips, stride=2 * block), :].astype(jnp.bfloat16)
                first = block + ((1 - core) * SLOTS + s) * chunks + j
                grad[at] = scr[pl.ds(first, chips, stride=2 * block), :].astype(jnp.bfloat16)
    per = lat.shape[0] // 3
    slots_per = per // chips
    for m in range(3):
        at = pl.ds(m * per, per)
        act = jnp.maximum(dot(lat[at, :], up_ref[...]), 0.0)
        squared = jnp.square(act).astype(jnp.bfloat16)
        out = dot(squared, down_ref[...])
        grad_act = contract_last(grad[at, :], down_ref[...])
        grad_pre = (2.0 * act * grad_act).astype(jnp.bfloat16)
        back = contract_last(grad_pre, up_ref[...])
        for q in range(slots_per):
            core, s = divmod(m * slots_per + q, SLOTS)
            for j in range(chunks):
                part = (slice(q * chips, (q + 1) * chips), slice(j * LANES, (j + 1) * LANES))
                first = core * block + s * chunks + j
                scr[pl.ds(first, chips, stride=2 * block), :] = out[part]
                scr[pl.ds(first + block // 2, chips, stride=2 * block), :] = back[part]
    out_ref[...] = scr[...].astype(jnp.bfloat16)


def finish_kernel(
    experts, core_ref, in_ref, high_ref, low_ref, mine_ref, other_ref, layer_ref, grad_ref, scr, rows
):
    chunks = rows.shape[1] // (2 * LANES)
    block = 2 * SLOTS * chunks
    scr[...] = in_ref[...].astype(jnp.float32)
    for s in range(SLOTS):
        for kind in range(2):
            for j in range(chunks):
                first = (kind * SLOTS + s) * chunks + j
                at = (pl.ds(s * experts, experts), pl.ds((kind * chunks + j) * LANES, LANES))
                rows[at] = scr[pl.ds(first, experts, stride=block), :].astype(jnp.bfloat16)
    total = dot(high_ref[...], rows[...]) + dot(low_ref[...], rows[...])
    total = total.astype(jnp.bfloat16)
    width = chunks * LANES
    combined, grad_sum = total[:, :width], total[:, width:]
    even = core_ref[0] == 0
    mine = contract_last(jnp.where(even, grad_sum, combined), whole_weight(mine_ref))
    other = contract_last(jnp.where(even, combined, grad_sum), whole_weight(other_ref))
    layer_ref[...] = jnp.where(even, other, mine).astype(jnp.bfloat16)
    grad_ref[...] = jnp.where(even, mine, other).astype(jnp.bfloat16)


def on_device(tokens, expert_ids, gate_values, latent_down, latent_up, expert_up, expert_down, grad_out):
    ep = lax.axis_size("ep")
    tok, wide = tokens.shape
    shard, width = latent_down.shape
    hidden = expert_up.shape[2]
    chunks = width // LANES
    block = 2 * SLOTS * chunks
    core = lax.axis_index("ep") % 2
    swap = [(i, i ^ 1) for i in range(ep)]
    bf16, f32 = jnp.bfloat16, jnp.float32

    def chunked(rows):
        return rows.reshape(shard, chunks, LANES).transpose(1, 0, 2).reshape(chunks * shard, LANES)

    both = jnp.stack([chunked(latent_down), chunked(latent_up.T)])
    cast = jnp.broadcast_to(both[None], (ep // 2, 2, chunks * shard, LANES))
    role = lax.all_to_all(
        cast.reshape(ep, chunks * shard, LANES), "ep", split_axis=0, concat_axis=0, tiled=True
    )

    even = core == 0
    own = jnp.where(even, tokens, grad_out)
    other = lax.ppermute(jnp.where(even, grad_out, tokens), "ep", swap)
    own_ids = expert_ids.T
    other_ids = lax.ppermute(own_ids, "ep", swap)

    place, high, low = vmem_call(
        functools.partial(route_kernel, ep),
        (
            jax.ShapeDtypeStruct((2 * SLOTS, ep, tok), bf16),
            jax.ShapeDtypeStruct((tok, SLOTS * ep), bf16),
            jax.ShapeDtypeStruct((tok, SLOTS * ep), bf16),
        ),
        [],
        8,
        4 * tok * tok * ep,
        MIB,
    )(own_ids, other_ids, gate_values.T)

    outbound = vmem_call(
        functools.partial(send_kernel, ep),
        jax.ShapeDtypeStruct((ep * block, LANES), bf16),
        [pltpu.VMEM((ep * block, LANES), f32)],
        24,
        4 * tok * wide * width,
        6 * MIB,
    )(own, other, role, place)

    arrived = lax.all_to_all(
        outbound.reshape(ep, block, LANES), "ep", split_axis=0, concat_axis=0, tiled=True
    )
    role_other = lax.ppermute(role, "ep", swap)

    rows = ep // 2 * 2 * SLOTS
    done = vmem_call(
        functools.partial(expert_kernel, ep // 2),
        jax.ShapeDtypeStruct((ep * block, LANES), bf16),
        [
            pltpu.VMEM((ep * block, LANES), f32),
            pltpu.VMEM((rows, width), bf16),
            pltpu.VMEM((rows, width), bf16),
        ],
        40,
        8 * rows * width * hidden,
        8 * MIB,
    )(arrived.reshape(ep * block, LANES), expert_up[0], expert_down[0])

    returned = lax.all_to_all(
        done.reshape(ep, block, LANES), "ep", split_axis=0, concat_axis=0, tiled=True
    )
    return pl.pallas_call(
        functools.partial(finish_kernel, ep),
        out_shape=(
            jax.ShapeDtypeStruct((tok, wide), bf16),
            jax.ShapeDtypeStruct((tok, wide), bf16),
        ),
        in_specs=[pl.BlockSpec(memory_space=pltpu.SMEM)]
        + [pl.BlockSpec(memory_space=pltpu.VMEM)] * 5,
        scratch_shapes=[
            pltpu.VMEM((ep * block, LANES), f32),
            pltpu.VMEM((SLOTS * ep, 2 * width), bf16),
        ],
        compiler_params=pltpu.CompilerParams(vmem_limit_bytes=32 * MIB),
        cost_estimate=pl.CostEstimate(
            flops=4 * tok * wide * width, bytes_accessed=7 * MIB, transcendentals=0
        ),
    )(core.reshape(1).astype(jnp.int32), returned.reshape(ep * block, LANES), high, low, role, role_other)


def solution(mesh):
    rows = P(("dp", "ep"), None)
    experts = P("ep", None, None)
    return jax.shard_map(
        on_device,
        mesh=mesh,
        in_specs=(rows, rows, rows, P("ep", None), P(None, "ep"), experts, experts, rows),
        out_specs=(rows, rows),
        check_vma=False,
    )
```

time: 343 us -> 193 us (0.56)
  waiting for transfers between devices: 250 us -> 80.4 us
  blocking collectives: 0 us -> 50.1 us
  matrix products: 22.1 us -> 0 us
  Pallas kernels: 0 us -> 16.5 us
  between operations: 14.2 us -> 0.79 us
  local copies, waits for them, and re-layouts: 15.9 us -> 8.79 us
  other arithmetic: 8.04 us -> 1.13 us
    all_gather x2 -> x0, waiting for transfers between devices: 169 us -> none  [the longest x1 87.9 us: on_device(): lax.all_gather(latent_down, 'ep', axis=0, tiled=True)]
    all_to_all x0 -> x1, blocking collectives: none -> 50.1 us  [on_device(): lax.all_to_all(outbound.reshape(ep, block, LANES), 'ep', split_axis=0, co...]
    dot_general x8 -> x0, matrix products: 22.1 us -> none  [the longest x1 5.44 us: on_device(): jnp.einsum('sjmf,jlf->sjml', grad_pre, expert_up, preferred_element_type=...]
    pallas_call x0 -> x4, Pallas kernels: none -> 16.5 us  [the longest x1 8.46 us: on_device(): vmem_call(functools.partial(expert_kernel, ep // 2), jax.ShapeDtypeStruct...]
    gather x4 -> x0, local copies, waits for them, and re-layouts: 7.62 us -> none  [the longest x2 4.74 us: on_device(): gathered_rows = jnp.take(returned, flat_slot, axis=0)]
    ppermute x0 -> x3, starting transfers between devices: none -> 7.59 us  [the longest x1 2.87 us: on_device(): role_other = lax.ppermute(role, 'ep', swap)]
    reduce_sum x5 -> x0, other arithmetic: 6.43 us -> none  [the longest x1 1.92 us: on_device(): jnp.sum(gate_values[:, :, None] * gathered_rows.astype(jnp.float32), axis=1)]
    all_to_all x4 -> x2, starting transfers between devices: 32.4 us -> 26.6 us  [the longest x1 18.6 us: on_device(): lax.all_to_all(cast.reshape(ep, chunks * shard, LANES), 'ep', split_axis=...]
  transfers between devices with their start and end apart: 6 -> 5, of which waited for: 5 -> 4; matrix products, arithmetic and copies ran while one was open for 8% -> 1% of each run, Pallas kernels for 0% -> 0%
where the time goes in v1:
time: 193 us; the launch traced here: 192 us
  waiting for transfers between devices  80.4 us (42%)
  blocking collectives  50.1 us (26%)
  starting transfers between devices  34.2 us (18%)
  Pallas kernels  16.5 us (9%)
  local copies, waits for them, and re-layouts  8.79 us (5%)
    all_to_all x1, blocking collectives, on_device(): lax.all_to_all(outbound.reshape(ep, block, LANES), 'ep', split_axis=0, co...  50.1 us
    all_to_all x1, waiting for transfers between devices, on_device(): lax.all_to_all(cast.reshape(ep, chunks * shard, LANES), 'ep', split_axis=...  42.5 us
    all_to_all x1, waiting for transfers between devices, on_device(): lax.all_to_all(done.reshape(ep, block, LANES), 'ep', split_axis=0, concat...  33 us
    all_to_all x1, starting transfers between devices, on_device(): lax.all_to_all(cast.reshape(ep, chunks * shard, LANES), 'ep', split_axis=...  18.6 us
    pallas_call x1, Pallas kernels, on_device(): vmem_call(functools.partial(expert_kernel, ep // 2), jax.ShapeDtypeStruct...  8.46 us
    all_to_all x1, starting transfers between devices, on_device(): lax.all_to_all(done.reshape(ep, block, LANES), 'ep', split_axis=0, concat...  8.06 us
    pallas_call x1, Pallas kernels, on_device(): pl.pallas_call(functools.partial(finish_kernel, ep), out_shape=(jax.Shape...  5.64 us
    unnamed x24, local copies, waits for them, and re-layouts  5.46 us
  transfers between devices with their start and end apart: 5, of which 4 were waited for; matrix products, arithmetic and copies ran while one was open for 1% of the time, Pallas kernels for 0%

profile of v1, /device:TPU:1, one launch (start us, length us, event | category | flops | bytes accessed | tf_op | source)
XLA Modules:
  0.0 191.9 jit_solution(2568408641331090961)
XLA Ops:
  0.6 0.7 reshape.30
  1.4 0.7 reshape.31
  2.1 1.9 broadcast_in_dim.2
  4.0 18.6 %all-to-all-start = ((bf16[128,64,128]{2,1,0:T(8,128)(2,1)}), bf16[128,64,128]{2,1,0:T(8,128)(2,1)S(1)}, u32[]{:S(2)}, u32[]{:S(2)}) async-start(bf16[128,64,128]{2,1,0:T(8,128)(2,1)} %bitcast.23), calls=%async_computation | async-start | bytes 4194304 | tf_op jit(solution)/shard_map/all_to_all | solution.py:159
  22.6 1.1 broadcast_select_fusion
  23.7 2.8 %collective-permute-start = (bf16[128,2048]{1,0:T(8,128)(2,1)S(1)}, bf16[128,2048]{1,0:T(8,128)(2,1)S(1)}, u32[]{:S(2)}, u32[]{:S(2)}) collective-permute-start(bf16[128,2048]{1,0:T(8,128)(2,1)S(1)} %get-tuple-element.8), channel_id=1, source_target_pairs={{0,4},{4,0},{8,12},{12,8},{16,20},{20,16},{24,28},{28,24},{32,36},... | collective-permute-start | bytes 1572872 | tf_op jit(solution)/shard_map/ppermute | solution.py:165
  26.5 1.9 %collective-permute-start.1 = (s32[4,128]{1,0:T(4,128)S(1)}, s32[4,128]{1,0:T(4,128)S(1)}, u32[]{:S(2)}, u32[]{:S(2)}) collective-permute-start(s32[4,128]{1,0:T(4,128)S(1)} %bitcast.20), channel_id=1, source_target_pairs={{0,4},{4,0},{8,12},{12,8},{16,20},{20,16},{24,28},{28,24},{32,36},... | collective-permute-start | bytes 6152 | tf_op jit(solution)/shard_map/ppermute | solution.py:167
  28.5 1.1 collective-permute-done.1.other_ids
  29.6 0.3 shard_map.95
  29.9 0.0 copy-start.3
  29.9 0.7 copy-done.3
  30.6 0.7 copy-done.5
  31.3 42.5 %all-to-all-done.w_ref.mine_ref = bf16[128,64,128]{2,1,0:T(8,128)(2,1)S(1)} async-done(((bf16[128,64,128]{2,1,0:T(8,128)(2,1)}), bf16[128,64,128]{2,1,0:T(8,128)(2,1)S(1)}, u32[]{:S(2)}, u32[]{:S(2)}) %all-to-all-start) | async-done | bytes 2097184 | tf_op jit(solution)/shard_map/all_to_all | solution.py:159
  73.8 2.1 %shard_map.96 = bf16[6144,128]{1,0:T(8,128)(2,1)S(1)} custom-call(bf16[128,2048]{1,0:T(8,128)(2,1)S(1)} %get-tuple-element.9.own_ref, bf16[128,2048]{1,0:T(8,128)(2,1)S(1)} %collective-permute-done.other_ref, bf16[128,64,128]{2,1,0:T(8,128)(2,1)S(1)} %all-to-all-done.w_ref.mine_ref, bf16[12,128,128]{2,1,0:T(8,128)(2,1)S(1)} %get-tuple-element.5.place_ref), custom_call_target="tpu_custom_call" | custom-call | flops 536870912 | bytes 6291456 | tf_op jit(solution)/shard_map/pallas_call | solution.py:182
  75.9 50.1 %all_to_all.15 = bf16[128,48,128]{2,1,0:T(8,128)(2,1)S(1)} all-to-all(bf16[128,48,128]{2,1,0:T(8,128)(2,1)S(1)} %bitcast.15), channel_id=1, replica_groups=mesh['ep'=128,'dp'=4] {'ep'}, dimensions={0} | all-to-all | bytes 3145728 | tf_op jit(solution)/shard_map/all_to_all | solution.py:191
  126.1 8.5 %shard_map.97 = bf16[6144,128]{1,0:T(8,128)(2,1)S(1)} custom-call(bf16[6144,128]{1,0:T(8,128)(2,1)S(1)} %bitcast.17, bf16[512,1408]{1,0:T(8,128)(2,1)S(1)} %bitcast.18, bf16[1408,512]{1,0:T(8,128)(2,1)S(1)} %bitcast.19), custom_call_target="tpu_custom_call" | custom-call | flops 4429185024 | bytes 8388608 | tf_op jit(solution)/shard_map/pallas_call | solution.py:197
  134.6 1.1 copy-done.2
  135.7 8.1 %all-to-all-start.2 = ((bf16[128,48,128]{2,1,0:T(8,128)(2,1)}), bf16[128,48,128]{2,1,0:T(8,128)(2,1)}, u32[]{:S(2)}, u32[]{:S(2)}) async-start(bf16[128,48,128]{2,1,0:T(8,128)(2,1)} %bitcast.16), calls=%async_computation.2 | async-start | bytes 3145728 | tf_op jit(solution)/shard_map/all_to_all | solution.py:210
  143.8 2.9 %collective-permute-start.2 = (bf16[128,64,128]{2,1,0:T(8,128)(2,1)S(1)}, bf16[128,64,128]{2,1,0:T(8,128)(2,1)S(1)}, u32[]{:S(2)}, u32[]{:S(2)}) collective-permute-start(bf16[128,64,128]{2,1,0:T(8,128)(2,1)S(1)} %all-to-all-done.w_ref.mine_ref), channel_id=1, source_target_pairs={{0,4},{4,0},{8,12},{12,8},{16,20},{20,16},{24,28},{28,24},{32,36},... | collective-permute-start | bytes 6291464 | tf_op jit(solution)/shard_map/ppermute | solution.py:194
  146.6 3.8 %collective-permute-done.2.other_ref = bf16[128,64,128]{2,1,0:T(8,128)(2,1)S(1)} collective-permute-done((bf16[128,64,128]{2,1,0:T(8,128)(2,1)S(1)}, bf16[128,64,128]{2,1,0:T(8,128)(2,1)S(1)}, u32[]{:S(2)}, u32[]{:S(2)}) %collective-permute-start.2) | collective-permute-done | bytes 2097184 | tf_op jit(solution)/shard_map/ppermute | solution.py:194
  150.4 1.3 copy-done
  151.7 33.0 %all-to-all-done.2 = bf16[128,48,128]{2,1,0:T(8,128)(2,1)} async-done(((bf16[128,48,128]{2,1,0:T(8,128)(2,1)}), bf16[128,48,128]{2,1,0:T(8,128)(2,1)}, u32[]{:S(2)}, u32[]{:S(2)}) %all-to-all-start.2) | async-done | bytes 1572896 | tf_op jit(solution)/shard_map/all_to_all | solution.py:210
  184.7 1.6 copy-done.1
  186.3 5.6 %shard_map.98 = (bf16[128,2048]{1,0:T(8,128)(2,1)}, bf16[128,2048]{1,0:T(8,128)(2,1)}) custom-call(s32[1]{0:T(128)} %bitcast.core_ref, bf16[6144,128]{1,0:T(8,128)(2,1)} %bitcast.14.in_ref, bf16[128,768]{1,0:T(8,128)(2,1)S(1)} %copy-done.4, bf16[128,768]{1,0:T(8,128)(2,1)S(1)} %copy-done.6, bf16[128,64,128]{2,1,0:T(8,128)(2,1)S(1)} %all-to-all-done.w_ref.mine_ref, ...), custom_call_target="tpu_custom_call" | custom-call | flops 536870912 | bytes 7340032 | tf_op jit(solution)/shard_map/pallas_call | solution.py:213
  (22 shorter events, 0.1 us)
Async XLA Ops:
  4.0 18.6 %copy-start.11 = (bf16[128,2048]{1,0:T(8,128)(2,1)S(1)}, bf16[128,2048]{1,0:T(8,128)(2,1)}, u32[]{:S(2)}) copy-start(bf16[128,2048]{1,0:T(8,128)(2,1)} %param.15) | copy-start | bytes 1572868
  4.0 69.8 %all-to-all-start = ((bf16[128,64,128]{2,1,0:T(8,128)(2,1)}), bf16[128,64,128]{2,1,0:T(8,128)(2,1)S(1)}, u32[]{:S(2)}, u32[]{:S(2)}) async-start(bf16[128,64,128]{2,1,0:T(8,128)(2,1)} %bitcast.23), calls=%async_computation | async-start | bytes 4194304 | tf_op jit(solution)/shard_map/all_to_all | solution.py:159
  22.5 4.0 %copy-start.9 = (s32[128,4]{0,1:T(4,128)S(1)}, s32[128,4]{0,1:T(4,128)}, u32[]{:S(2)}) copy-start(s32[128,4]{0,1:T(4,128)} %param.9) | copy-start | bytes 6148
  22.6 7.0 %copy-start.10 = (f32[128,4]{0,1:T(4,128)S(1)}, f32[128,4]{0,1:T(4,128)}, u32[]{:S(2)}) copy-start(f32[128,4]{0,1:T(4,128)} %param.10) | copy-start | bytes 6148
  23.7 7.6 %collective-permute-start = (bf16[128,2048]{1,0:T(8,128)(2,1)S(1)}, bf16[128,2048]{1,0:T(8,128)(2,1)S(1)}, u32[]{:S(2)}, u32[]{:S(2)}) collective-permute-start(bf16[128,2048]{1,0:T(8,128)(2,1)S(1)} %get-tuple-element.8), channel_id=1, source_target_pairs={{0,4},{4,0},{8,12},{12,8},{16,20},{20,16},{24,28},{28,24},{32,36},... | collective-permute-start | bytes 1572872 | tf_op jit(solution)/shard_map/ppermute | solution.py:165
  26.5 3.1 %collective-permute-start.1 = (s32[4,128]{1,0:T(4,128)S(1)}, s32[4,128]{1,0:T(4,128)S(1)}, u32[]{:S(2)}, u32[]{:S(2)}) collective-permute-start(s32[4,128]{1,0:T(4,128)S(1)} %bitcast.20), channel_id=1, source_target_pairs={{0,4},{4,0},{8,12},{12,8},{16,20},{20,16},{24,28},{28,24},{32,36},... | collective-permute-start | bytes 6152 | tf_op jit(solution)/shard_map/ppermute | solution.py:167
  29.9 0.7 copy-start.3
  30.6 0.7 copy-start.5
  75.9 50.2 %copy-start.7 = (bf16[1,512,1408]{2,1,0:T(8,128)(2,1)S(1)}, bf16[1,512,1408]{2,1,0:T(8,128)(2,1)}, u32[]{:S(2)}) copy-start(bf16[1,512,1408]{2,1,0:T(8,128)(2,1)} %param.13) | copy-start | bytes 4325380
  75.9 50.1 %copy-start.8 = (bf16[1,1408,512]{2,1,0:T(8,128)(2,1)S(1)}, bf16[1,1408,512]{2,1,0:T(8,128)(2,1)}, u32[]{:S(2)}) copy-start(bf16[1,1408,512]{2,1,0:T(8,128)(2,1)} %param.14) | copy-start | bytes 4325380
  134.5 1.2 copy-start.2
  135.7 49.0 %copy-start.4 = (bf16[128,768]{1,0:T(8,128)(2,1)S(1)}, bf16[128,768]{1,0:T(8,128)(2,1)}, u32[]{:S(2)}) copy-start(bf16[128,768]{1,0:T(8,128)(2,1)} %copy-done.3) | copy-start | bytes 589828
  135.7 49.0 %copy-start.6 = (bf16[128,768]{1,0:T(8,128)(2,1)S(1)}, bf16[128,768]{1,0:T(8,128)(2,1)}, u32[]{:S(2)}) copy-start(bf16[128,768]{1,0:T(8,128)(2,1)} %copy-done.5) | copy-start | bytes 589828
  135.7 49.0 %all-to-all-start.2 = ((bf16[128,48,128]{2,1,0:T(8,128)(2,1)}), bf16[128,48,128]{2,1,0:T(8,128)(2,1)}, u32[]{:S(2)}, u32[]{:S(2)}) async-start(bf16[128,48,128]{2,1,0:T(8,128)(2,1)} %bitcast.16), calls=%async_computation.2 | async-start | bytes 3145728 | tf_op jit(solution)/shard_map/all_to_all | solution.py:210
  143.8 6.6 %collective-permute-start.2 = (bf16[128,64,128]{2,1,0:T(8,128)(2,1)S(1)}, bf16[128,64,128]{2,1,0:T(8,128)(2,1)S(1)}, u32[]{:S(2)}, u32[]{:S(2)}) collective-permute-start(bf16[128,64,128]{2,1,0:T(8,128)(2,1)S(1)} %all-to-all-done.w_ref.mine_ref), channel_id=1, source_target_pairs={{0,4},{4,0},{8,12},{12,8},{16,20},{20,16},{24,28},{28,24},{32,36},... | collective-permute-start | bytes 6291464 | tf_op jit(solution)/shard_map/ppermute | solution.py:194
  150.4 1.3 copy-start
  184.7 1.6 copy-start.1

commit v2 on v1

--- a/solution.py
+++ b/solution.py
@@ -22,10 +22,12 @@
     )
 
 
-def vmem_call(body, out_shape, scratch, limit_mib, flops, moved):
+def vmem_call(body, out_shape, scratch, limit_mib, flops, moved, arrays, scalars=0):
     return pl.pallas_call(
         body,
         out_shape=out_shape,
+        in_specs=[pl.BlockSpec(memory_space=pltpu.SMEM)] * scalars
+        + [pl.BlockSpec(memory_space=pltpu.VMEM)] * arrays,
         scratch_shapes=scratch,
         compiler_params=pltpu.CompilerParams(vmem_limit_bytes=limit_mib * MIB),
         cost_estimate=pl.CostEstimate(flops=flops, bytes_accessed=moved, transcendentals=0),
@@ -59,7 +61,16 @@
                 low_ref[:, at] = (gate - high.astype(jnp.float32)).astype(jnp.bfloat16)
 
 
-def whole_weight(w_ref):
+def cast_kernel(plane_ref, down_ref, up_ref, out_ref):
+    shard = jnp.where(plane_ref[0] == 0, down_ref[...], up_ref[...])
+    rows, width = shard.shape
+    for j in range(width // LANES):
+        piece = shard[:, j * LANES : (j + 1) * LANES]
+        at = pl.ds(j * rows, rows)
+        out_ref[:, at, :] = jnp.broadcast_to(piece[None], (out_ref.shape[0], rows, LANES))
+
+
+def half_weight(w_ref):
     shards, rows, lanes = w_ref.shape
     per = 16
     parts = [
@@ -69,16 +80,28 @@
     return jnp.concatenate(parts, axis=1)
 
 
-def send_kernel(experts, own_ref, other_ref, w_ref, place_ref, out_ref, scr):
-    tok = own_ref.shape[0]
-    weight = whole_weight(w_ref)
-    block = out_ref.shape[0] // experts
-    for half, x_ref in enumerate((own_ref, other_ref)):
-        latent = dot(x_ref[...], weight).astype(jnp.bfloat16)
+def project_kernel(a_ref, b_ref, c_ref, d_ref, w_ref, mine_ref, theirs_ref):
+    weight = half_weight(w_ref)
+    tok = a_ref.shape[0]
+    for n, x_ref in enumerate((a_ref, b_ref, c_ref, d_ref)):
+        out_ref = (mine_ref, theirs_ref)[n // 2]
+        out_ref[pl.ds(n % 2 * tok, tok), :] = dot(x_ref[...], weight).astype(jnp.bfloat16)
+
+
+def send_kernel(experts, plane_ref, mine_ref, swapped_ref, place_ref, out_ref, scr):
+    first_plane = plane_ref[0] == 0
+    mine, swapped = mine_ref[...], swapped_ref[...]
+    latent = jnp.where(first_plane, mine, swapped)
+    grad = jnp.where(first_plane, swapped, mine)
+    both = jnp.concatenate([latent, grad], axis=1)
+    tok = both.shape[0] // 2
+    chunks = both.shape[1] // LANES
+    block = 2 * SLOTS * chunks
+    for half in range(2):
         for s in range(SLOTS):
-            rows = dot(place_ref[half * SLOTS + s], latent)
-            for j in range(rows.shape[1] // LANES):
-                first = (half * SLOTS + s) * (rows.shape[1] // LANES) + j
+            rows = dot(place_ref[half * SLOTS + s], both[half * tok : (half + 1) * tok])
+            for j in range(chunks):
+                first = (half * SLOTS + s) * chunks + j
                 scr[pl.ds(first, experts, stride=block), :] = rows[:, j * LANES : (j + 1) * LANES]
     out_ref[...] = scr[...].astype(jnp.bfloat16)
 
@@ -90,12 +113,13 @@
     scr[...] = in_ref[...].astype(jnp.float32)
     for core in range(2):
         for s in range(SLOTS):
-            slot = core * SLOTS + s
             for j in range(chunks):
-                at = (pl.ds(slot * chips, chips), pl.ds(j * LANES, LANES))
-                first = (core * SLOTS + s) * chunks + j
+                sender, part = divmod(j, chunks // 2)
+                slot = s if sender == core else SLOTS + s
+                at = (pl.ds((core * SLOTS + s) * chips, chips), pl.ds(j * LANES, LANES))
+                first = sender * block + slot * chunks + part
                 lat[at] = scr[pl.ds(first, chips, stride=2 * block), :].astype(jnp.bfloat16)
-                first = block + ((1 - core) * SLOTS + s) * chunks + j
+                first += chunks // 2
                 grad[at] = scr[pl.ds(first, chips, stride=2 * block), :].astype(jnp.bfloat16)
     per = lat.shape[0] // 3
     slots_per = per // chips
@@ -117,9 +141,26 @@
     out_ref[...] = scr[...].astype(jnp.bfloat16)
 
 
-def finish_kernel(
-    experts, core_ref, in_ref, high_ref, low_ref, mine_ref, other_ref, layer_ref, grad_ref, scr, rows
-):
+def weight_kernel(place_ref, same_ref, next_ref, plane_ref, far_ref, down_ref, up_ref):
+    first_plane, first_core = place_ref[0] == 0, place_ref[1] == 0
+    half = down_ref.shape[1] // 2
+    per = 16
+    for j in range(half // LANES):
+        rows = slice(j * per, (j + 1) * per)
+
+        def piece(ref):
+            return ref[:, rows, :].reshape(-1, LANES)
+
+        same, beside, plane, far = piece(same_ref), piece(next_ref), piece(plane_ref), piece(far_ref)
+        for low in range(2):
+            mine = jnp.where(first_core, (same, beside)[low], (beside, same)[low])
+            theirs = jnp.where(first_core, (plane, far)[low], (far, plane)[low])
+            at = pl.ds(low * half + j * LANES, LANES)
+            down_ref[:, at] = jnp.where(first_plane, mine, theirs)
+            up_ref[:, at] = jnp.where(first_plane, theirs, mine)
+
+
+def finish_kernel(experts, in_ref, high_ref, low_ref, down_ref, up_ref, layer_ref, grad_ref, scr, rows):
     chunks = rows.shape[1] // (2 * LANES)
     block = 2 * SLOTS * chunks
     scr[...] = in_ref[...].astype(jnp.float32)
@@ -132,39 +173,47 @@
     total = dot(high_ref[...], rows[...]) + dot(low_ref[...], rows[...])
     total = total.astype(jnp.bfloat16)
     width = chunks * LANES
-    combined, grad_sum = total[:, :width], total[:, width:]
-    even = core_ref[0] == 0
-    mine = contract_last(jnp.where(even, grad_sum, combined), whole_weight(mine_ref))
-    other = contract_last(jnp.where(even, combined, grad_sum), whole_weight(other_ref))
-    layer_ref[...] = jnp.where(even, other, mine).astype(jnp.bfloat16)
-    grad_ref[...] = jnp.where(even, mine, other).astype(jnp.bfloat16)
+    layer_ref[...] = contract_last(total[:, :width], up_ref[...]).astype(jnp.bfloat16)
+    grad_ref[...] = contract_last(total[:, width:], down_ref[...]).astype(jnp.bfloat16)
 
 
 def on_device(tokens, expert_ids, gate_values, latent_down, latent_up, expert_up, expert_down, grad_out):
-    ep = lax.axis_size("ep")
+    ep, dp = lax.axis_size("ep"), lax.axis_size("dp")
     tok, wide = tokens.shape
     shard, width = latent_down.shape
     hidden = expert_up.shape[2]
     chunks = width // LANES
     block = 2 * SLOTS * chunks
-    core = lax.axis_index("ep") % 2
-    swap = [(i, i ^ 1) for i in range(ep)]
+    core = (lax.axis_index("ep") % 2).astype(jnp.int32)
+    plane = (lax.axis_index("dp") % 2).astype(jnp.int32)
+    place_of = jnp.stack([plane, core])
     bf16, f32 = jnp.bfloat16, jnp.float32
 
-    def chunked(rows):
-        return rows.reshape(shard, chunks, LANES).transpose(1, 0, 2).reshape(chunks * shard, LANES)
-
-    both = jnp.stack([chunked(latent_down), chunked(latent_up.T)])
-    cast = jnp.broadcast_to(both[None], (ep // 2, 2, chunks * shard, LANES))
-    role = lax.all_to_all(
-        cast.reshape(ep, chunks * shard, LANES), "ep", split_axis=0, concat_axis=0, tiled=True
-    )
-
-    even = core == 0
-    own = jnp.where(even, tokens, grad_out)
-    other = lax.ppermute(jnp.where(even, grad_out, tokens), "ep", swap)
+    def beside(x):
+        return lax.ppermute(x, "ep", [(i, i ^ 1) for i in range(ep)])
+
+    def next_plane(x):
+        return lax.ppermute(x, "dp", [(i, i ^ 1) for i in range(dp)])
+
+    def exchange(x):
+        return lax.all_to_all(x, "ep", split_axis=0, concat_axis=0, tiled=True)
+
+    cast = vmem_call(
+        cast_kernel,
+        jax.ShapeDtypeStruct((ep // 2, chunks * shard, LANES), bf16),
+        [],
+        8,
+        0,
+        MIB,
+        scalars=1,
+        arrays=2,
+    )(place_of, latent_down, latent_up.T)
+    same = exchange(cast.reshape(ep, chunks // 2 * shard, LANES))
+
+    first_plane = plane == 0
+    own = jnp.where(first_plane, tokens, grad_out)
+    theirs = next_plane(jnp.where(first_plane, grad_out, tokens))
     own_ids = expert_ids.T
-    other_ids = lax.ppermute(own_ids, "ep", swap)
 
     place, high, low = vmem_call(
         functools.partial(route_kernel, ep),
@@ -177,21 +226,33 @@
         8,
         4 * tok * tok * ep,
         MIB,
-    )(own_ids, other_ids, gate_values.T)
+        arrays=3,
+    )(own_ids, beside(own_ids), gate_values.T)
+
+    projected = jax.ShapeDtypeStruct((2 * tok, width // 2), bf16)
+    mine, away = vmem_call(
+        project_kernel,
+        (projected, projected),
+        [],
+        12,
+        4 * tok * wide * width,
+        4 * MIB,
+        arrays=5,
+    )(own, beside(own), theirs, beside(theirs), same)
 
     outbound = vmem_call(
         functools.partial(send_kernel, ep),
         jax.ShapeDtypeStruct((ep * block, LANES), bf16),
         [pltpu.VMEM((ep * block, LANES), f32)],
-        24,
-        4 * tok * wide * width,
-        6 * MIB,
-    )(own, other, role, place)
-
-    arrived = lax.all_to_all(
-        outbound.reshape(ep, block, LANES), "ep", split_axis=0, concat_axis=0, tiled=True
-    )
-    role_other = lax.ppermute(role, "ep", swap)
+        12,
+        4 * SLOTS * tok * ep * width,
+        3 * MIB,
+        scalars=1,
+        arrays=3,
+    )(place_of, mine, next_plane(away), place)
+
+    arrived = exchange(outbound.reshape(ep, block, LANES))
+    other = next_plane(same)
 
     rows = ep // 2 * 2 * SLOTS
     done = vmem_call(
@@ -202,31 +263,30 @@
             pltpu.VMEM((rows, width), bf16),
             pltpu.VMEM((rows, width), bf16),
         ],
-        40,
+        32,
         8 * rows * width * hidden,
         8 * MIB,
+        arrays=3,
     )(arrived.reshape(ep * block, LANES), expert_up[0], expert_down[0])
 
-    returned = lax.all_to_all(
-        done.reshape(ep, block, LANES), "ep", split_axis=0, concat_axis=0, tiled=True
-    )
-    return pl.pallas_call(
+    returned = exchange(done.reshape(ep, block, LANES))
+    whole = jax.ShapeDtypeStruct((wide, width), bf16)
+    down, up = vmem_call(
+        weight_kernel, (whole, whole), [], 16, 0, 8 * MIB, scalars=1, arrays=4
+    )(place_of, same, beside(same), other, beside(other))
+    result = jax.ShapeDtypeStruct((tok, wide), bf16)
+    return vmem_call(
         functools.partial(finish_kernel, ep),
-        out_shape=(
-            jax.ShapeDtypeStruct((tok, wide), bf16),
-            jax.ShapeDtypeStruct((tok, wide), bf16),
-        ),
-        in_specs=[pl.BlockSpec(memory_space=pltpu.SMEM)]
-        + [pl.BlockSpec(memory_space=pltpu.VMEM)] * 5,
-        scratch_shapes=[
+        (result, result),
+        [
             pltpu.VMEM((ep * block, LANES), f32),
             pltpu.VMEM((SLOTS * ep, 2 * width), bf16),
         ],
-        compiler_params=pltpu.CompilerParams(vmem_limit_bytes=32 * MIB),
-        cost_estimate=pl.CostEstimate(
-            flops=4 * tok * wide * width, bytes_accessed=7 * MIB, transcendentals=0
-        ),
-    )(core.reshape(1).astype(jnp.int32), returned.reshape(ep * block, LANES), high, low, role, role_other)
+        20,
+        4 * tok * wide * width,
+        7 * MIB,
+        arrays=5,
+    )(returned.reshape(ep * block, LANES), high, low, down, up)
 
 
 def solution(mesh):

time: 193 us -> 178 us (0.922)
  waiting for transfers between devices: 80.4 us -> 48 us
  starting transfers between devices: 34.2 us -> 51.6 us
  Pallas kernels: 16.5 us -> 19.2 us
    all_to_all x2, waiting for transfers between devices: 75.5 us -> 16 us  [exchange(): return lax.all_to_all(x, 'ep', split_axis=0, concat_axis=0, tiled=True)]
    ppermute x3 -> x8, waiting for transfers between devices: 4.89 us -> 32 us  [the longest x3 27.7 us: next_plane(): return lax.ppermute(x, 'dp', [(i, i ^ 1) for i in range(dp)])]
    ppermute x3 -> x8, starting transfers between devices: 7.59 us -> 25.6 us  [the longest x5 16.2 us: beside(): return lax.ppermute(x, 'ep', [(i, i ^ 1) for i in range(ep)])]
    unnamed x24 -> x26, local copies, waits for them, and re-layouts: 5.46 us -> 8.46 us
    pallas_call x1 -> x4, Pallas kernels: 5.64 us -> 8.61 us  [the longest x1 3.98 us: on_device(): vmem_call(functools.partial(finish_kernel, ep), (result, result), [pltpu....]
  transfers between devices with their start and end apart: 5 -> 10, of which waited for: 4 -> 7; matrix products, arithmetic and copies ran while one was open for 1% -> 0% of each run, Pallas kernels for 0% -> 1%
where the time goes in v2:
time: 178 us; the launch traced here: 176 us
  starting transfers between devices  51.6 us (29%)
  blocking collectives  48.2 us (27%)
  waiting for transfers between devices  48 us (27%)
  Pallas kernels  19.2 us (11%)
  local copies, waits for them, and re-layouts  8.46 us (5%)
    all_to_all x1, blocking collectives, exchange(): return lax.all_to_all(x, 'ep', split_axis=0, concat_axis=0, tiled=True)  48.2 us
    ppermute x3, waiting for transfers between devices, next_plane(): return lax.ppermute(x, 'dp', [(i, i ^ 1) for i in range(dp)])  27.7 us
    all_to_all x2, starting transfers between devices, exchange(): return lax.all_to_all(x, 'ep', split_axis=0, concat_axis=0, tiled=True)  26 us
    ppermute x5, starting transfers between devices, beside(): return lax.ppermute(x, 'ep', [(i, i ^ 1) for i in range(ep)])  16.2 us
    all_to_all x2, waiting for transfers between devices, exchange(): return lax.all_to_all(x, 'ep', split_axis=0, concat_axis=0, tiled=True)  16 us
    ppermute x3, starting transfers between devices, next_plane(): return lax.ppermute(x, 'dp', [(i, i ^ 1) for i in range(dp)])  9.35 us
    unnamed x26, local copies, waits for them, and re-layouts  8.46 us
    pallas_call x1, Pallas kernels, on_device(): vmem_call(functools.partial(expert_kernel, ep // 2), jax.ShapeDtypeStruct...  8.42 us
  transfers between devices with their start and end apart: 10, of which 7 were waited for; matrix products, arithmetic and copies ran while one was open for 0% of the time, Pallas kernels for 1%

profile of v2, /device:TPU:1, one launch (start us, length us, event | category | flops | bytes accessed | tf_op | source)
XLA Modules:
  0.0 176.4 jit_solution(17632843210113531267)
XLA Ops:
  2.2 1.8 %shard_map.95 = bf16[64,64,128]{2,1,0:T(8,128)(2,1)} custom-call(s32[2]{0:T(128)S(1)} %pad_add_fusion.plane_ref.place_ref, bf16[16,512]{1,0:T(8,128)(2,1)S(1)} %copy-done.5, bf16[16,512]{1,0:T(8,128)(2,1)S(1)} %bitcast.16), custom_call_target="tpu_custom_call" | custom-call | bytes 1048576 | tf_op jit(solution)/shard_map/pallas_call | solution.py:201
  4.0 18.4 %all-to-all-start = ((bf16[128,32,128]{2,1,0:T(8,128)(2,1)}), bf16[128,32,128]{2,1,0:T(8,128)(2,1)S(1)}, u32[]{:S(2)}, u32[]{:S(2)}) async-start(bf16[128,32,128]{2,1,0:T(8,128)(2,1)} %bitcast.3), calls=%async_computation | async-start | bytes 2097152 | tf_op jit(solution)/shard_map/all_to_all | solution.py:199
  22.5 3.1 %collective-permute-start.1 = (bf16[128,2048]{1,0:T(8,128)(2,1)S(1)}, bf16[128,2048]{1,0:T(8,128)(2,1)S(1)}, u32[]{:S(2)}, u32[]{:S(2)}) collective-permute-start(bf16[128,2048]{1,0:T(8,128)(2,1)S(1)} %get-tuple-element.16), channel_id=1, source_target_pairs={{0,1},{1,0},{2,3},{3,2},{4,5},{5,4},{6,7},{7,6},{8,9},{9,8},{10,11... | collective-permute-start | bytes 1572872 | tf_op jit(solution)/shard_map/ppermute | solution.py:196
  25.7 3.1 %collective-permute-start = (bf16[128,2048]{1,0:T(8,128)(2,1)S(1)}, bf16[128,2048]{1,0:T(8,128)(2,1)S(1)}, u32[]{:S(2)}, u32[]{:S(2)}) collective-permute-start(bf16[128,2048]{1,0:T(8,128)(2,1)S(1)} %get-tuple-element.17.a_ref), channel_id=1, source_target_pairs={{0,4},{4,0},{8,12},{12,8},{16,20},{20,16},{24,28},{28,24},{32,36},... | collective-permute-start | bytes 1572872 | tf_op jit(solution)/shard_map/ppermute | solution.py:193
  28.7 8.2 %collective-permute-done.1.c_ref = bf16[128,2048]{1,0:T(8,128)(2,1)S(1)} collective-permute-done((bf16[128,2048]{1,0:T(8,128)(2,1)S(1)}, bf16[128,2048]{1,0:T(8,128)(2,1)S(1)}, u32[]{:S(2)}, u32[]{:S(2)}) %collective-permute-start.1) | collective-permute-done | bytes 524320 | tf_op jit(solution)/shard_map/ppermute | solution.py:196
  36.9 3.7 %collective-permute-start.2 = (bf16[128,2048]{1,0:T(8,128)(2,1)S(1)}, bf16[128,2048]{1,0:T(8,128)(2,1)S(1)}, u32[]{:S(2)}, u32[]{:S(2)}) collective-permute-start(bf16[128,2048]{1,0:T(8,128)(2,1)S(1)} %collective-permute-done.1.c_ref), channel_id=1, source_target_pairs={{0,4},{4,0},{8,12},{12,8},{16,20},{20,16},{24,28},{28,24},{32,36},... | collective-permute-start | bytes 1572872 | tf_op jit(solution)/shard_map/ppermute | solution.py:193
  40.7 1.5 collective-permute-done.2.d_ref
  42.2 11.1 %all-to-all-done.w_ref.same_ref = bf16[128,32,128]{2,1,0:T(8,128)(2,1)S(1)} async-done(((bf16[128,32,128]{2,1,0:T(8,128)(2,1)}), bf16[128,32,128]{2,1,0:T(8,128)(2,1)S(1)}, u32[]{:S(2)}, u32[]{:S(2)}) %all-to-all-start) | async-done | bytes 1048608 | tf_op jit(solution)/shard_map/all_to_all | solution.py:199
  54.0 3.1 %collective-permute-start.3 = (bf16[256,256]{1,0:T(8,128)(2,1)S(1)}, bf16[256,256]{1,0:T(8,128)(2,1)S(1)}, u32[]{:S(2)}, u32[]{:S(2)}) collective-permute-start(bf16[256,256]{1,0:T(8,128)(2,1)S(1)} %get-tuple-element.10), channel_id=1, source_target_pairs={{0,1},{1,0},{2,3},{3,2},{4,5},{5,4},{6,7},{7,6},{8,9},{9,8},{10,11... | collective-permute-start | bytes 393224 | tf_op jit(solution)/shard_map/ppermute | solution.py:196
  57.2 2.5 %collective-permute-start.4 = (s32[4,128]{1,0:T(4,128)S(1)}, s32[4,128]{1,0:T(4,128)S(1)}, u32[]{:S(2)}, u32[]{:S(2)}) collective-permute-start(s32[4,128]{1,0:T(4,128)S(1)} %bitcast.19), channel_id=1, source_target_pairs={{0,4},{4,0},{8,12},{12,8},{16,20},{20,16},{24,28},{28,24},{32,36},... | collective-permute-start | bytes 6152 | tf_op jit(solution)/shard_map/ppermute | solution.py:193
  60.8 1.8 %shard_map.98 = bf16[6144,128]{1,0:T(8,128)(2,1)S(1)} custom-call(s32[2]{0:T(128)S(1)} %pad_add_fusion.plane_ref.place_ref, bf16[256,256]{1,0:T(8,128)(2,1)S(1)} %get-tuple-element.9.mine_ref, bf16[256,256]{1,0:T(8,128)(2,1)S(1)} %collective-permute-done.3.swapped_ref, bf16[12,128,128]{2,1,0:T(8,128)(2,1)S(1)} %get-tuple-element.11.place_ref), custom_call_target="tpu_custom_call" | custom-call | flops 201326592 | bytes 3145728 | tf_op jit(solution)/shard_map/pallas_call | solution.py:243
  62.6 48.2 %all_to_all.15 = bf16[128,48,128]{2,1,0:T(8,128)(2,1)S(1)} all-to-all(bf16[128,48,128]{2,1,0:T(8,128)(2,1)S(1)} %bitcast.12), channel_id=1, replica_groups=mesh['ep'=128,'dp'=4] {'ep'}, dimensions={0} | all-to-all | bytes 3145728 | tf_op jit(solution)/shard_map/all_to_all | solution.py:199
  110.9 8.4 %shard_map.99 = bf16[6144,128]{1,0:T(8,128)(2,1)S(1)} custom-call(bf16[6144,128]{1,0:T(8,128)(2,1)S(1)} %bitcast.15, bf16[512,1408]{1,0:T(8,128)(2,1)S(1)} %bitcast.17, bf16[1408,512]{1,0:T(8,128)(2,1)S(1)} %bitcast.18), custom_call_target="tpu_custom_call" | custom-call | flops 4429185024 | bytes 8388608 | tf_op jit(solution)/shard_map/pallas_call | solution.py:258
  120.5 7.5 %all-to-all-start.2 = ((bf16[128,48,128]{2,1,0:T(8,128)(2,1)}), bf16[128,48,128]{2,1,0:T(8,128)(2,1)S(1)}, u32[]{:S(2)}, u32[]{:S(2)}) async-start(bf16[128,48,128]{2,1,0:T(8,128)(2,1)} %bitcast.14), calls=%async_computation.2 | async-start | bytes 3145728 | tf_op jit(solution)/shard_map/all_to_all | solution.py:199
  128.0 3.1 %collective-permute-start.6 = (bf16[128,32,128]{2,1,0:T(8,128)(2,1)S(1)}, bf16[128,32,128]{2,1,0:T(8,128)(2,1)S(1)}, u32[]{:S(2)}, u32[]{:S(2)}) collective-permute-start(bf16[128,32,128]{2,1,0:T(8,128)(2,1)S(1)} %all-to-all-done.w_ref.same_ref), channel_id=1, source_target_pairs={{0,1},{1,0},{2,3},{3,2},{4,5},{5,4},{6,7},{7,6},{8,9},{9,8},{10,11... | collective-permute-start | bytes 3145736 | tf_op jit(solution)/shard_map/ppermute | solution.py:196
  131.1 3.1 %collective-permute-start.5 = (bf16[128,32,128]{2,1,0:T(8,128)(2,1)S(1)}, bf16[128,32,128]{2,1,0:T(8,128)(2,1)S(1)}, u32[]{:S(2)}, u32[]{:S(2)}) collective-permute-start(bf16[128,32,128]{2,1,0:T(8,128)(2,1)S(1)} %all-to-all-done.w_ref.same_ref), channel_id=1, source_target_pairs={{0,4},{4,0},{8,12},{12,8},{16,20},{20,16},{24,28},{28,24},{32,36},... | collective-permute-start | bytes 3145736 | tf_op jit(solution)/shard_map/ppermute | solution.py:193
  134.2 19.5 %collective-permute-done.6.plane_ref = bf16[128,32,128]{2,1,0:T(8,128)(2,1)S(1)} collective-permute-done((bf16[128,32,128]{2,1,0:T(8,128)(2,1)S(1)}, bf16[128,32,128]{2,1,0:T(8,128)(2,1)S(1)}, u32[]{:S(2)}, u32[]{:S(2)}) %collective-permute-start.6) | collective-permute-done | bytes 1048608 | tf_op jit(solution)/shard_map/ppermute | solution.py:196
  153.7 3.9 %collective-permute-start.7 = (bf16[128,32,128]{2,1,0:T(8,128)(2,1)S(1)}, bf16[128,32,128]{2,1,0:T(8,128)(2,1)S(1)}, u32[]{:S(2)}, u32[]{:S(2)}) collective-permute-start(bf16[128,32,128]{2,1,0:T(8,128)(2,1)S(1)} %collective-permute-done.6.plane_ref), channel_id=1, source_target_pairs={{0,4},{4,0},{8,12},{12,8},{16,20},{20,16},{24,28},{28,24},{32,36},... | collective-permute-start | bytes 3145736 | tf_op jit(solution)/shard_map/ppermute | solution.py:193
  157.6 2.0 %collective-permute-done.7.far_ref = bf16[128,32,128]{2,1,0:T(8,128)(2,1)S(1)} collective-permute-done((bf16[128,32,128]{2,1,0:T(8,128)(2,1)S(1)}, bf16[128,32,128]{2,1,0:T(8,128)(2,1)S(1)}, u32[]{:S(2)}, u32[]{:S(2)}) %collective-permute-start.7) | collective-permute-done | bytes 1048608 | tf_op jit(solution)/shard_map/ppermute | solution.py:193
  159.7 2.1 %shard_map.100 = (bf16[2048,512]{1,0:T(8,128)(2,1)S(1)}, bf16[2048,512]{1,0:T(8,128)(2,1)S(1)}) custom-call(s32[2]{0:T(128)S(1)} %pad_add_fusion.plane_ref.place_ref, bf16[128,32,128]{2,1,0:T(8,128)(2,1)S(1)} %all-to-all-done.w_ref.same_ref, bf16[128,32,128]{2,1,0:T(8,128)(2,1)S(1)} %collective-permute-done.5.next_ref, ...), custom_call_target="tpu_custom_call" | custom-call | bytes 8388608 | tf_op jit(solution)/shard_map/pallas_call | solution.py:274
  164.4 4.8 %all-to-all-done.2 = bf16[128,48,128]{2,1,0:T(8,128)(2,1)S(1)} async-done(((bf16[128,48,128]{2,1,0:T(8,128)(2,1)}), bf16[128,48,128]{2,1,0:T(8,128)(2,1)S(1)}, u32[]{:S(2)}, u32[]{:S(2)}) %all-to-all-start.2) | async-done | bytes 1572896 | tf_op jit(solution)/shard_map/all_to_all | solution.py:199
  169.3 1.6 copy-done.1
  170.8 1.6 copy-done.3
  172.4 4.0 %shard_map.101 = (bf16[128,2048]{1,0:T(8,128)(2,1)}, bf16[128,2048]{1,0:T(8,128)(2,1)}) custom-call(bf16[6144,128]{1,0:T(8,128)(2,1)S(1)} %bitcast.13, bf16[128,768]{1,0:T(8,128)(2,1)S(1)} %get-tuple-element.12.high_ref, bf16[128,768]{1,0:T(8,128)(2,1)S(1)} %get-tuple-element.13.low_ref, bf16[2048,512]{1,0:T(8,128)(2,1)S(1)} %copy-done.1, ...), custom_call_target="tpu_custom_call" | custom-call | flops 536870912 | bytes 7340032 | tf_op jit(solution)/shard_map/pallas_call | solution.py:278
  (32 shorter events, 7.3 us)
Async XLA Ops:
  0.7 0.7 copy-start.5
  1.4 0.7 copy-start.6
  2.2 20.2 %copy-start.11 = (bf16[128,2048]{1,0:T(8,128)(2,1)S(1)}, bf16[128,2048]{1,0:T(8,128)(2,1)}, u32[]{:S(2)}) copy-start(bf16[128,2048]{1,0:T(8,128)(2,1)} %param.15) | copy-start | bytes 1572868
  2.2 20.3 %copy-start.12 = (bf16[128,2048]{1,0:T(8,128)(2,1)S(1)}, bf16[128,2048]{1,0:T(8,128)(2,1)}, u32[]{:S(2)}) copy-start(bf16[128,2048]{1,0:T(8,128)(2,1)} %param.8) | copy-start | bytes 1572868
  4.0 49.3 %all-to-all-start = ((bf16[128,32,128]{2,1,0:T(8,128)(2,1)}), bf16[128,32,128]{2,1,0:T(8,128)(2,1)S(1)}, u32[]{:S(2)}, u32[]{:S(2)}) async-start(bf16[128,32,128]{2,1,0:T(8,128)(2,1)} %bitcast.3), calls=%async_computation | async-start | bytes 2097152 | tf_op jit(solution)/shard_map/all_to_all | solution.py:199
  22.5 14.4 %collective-permute-start.1 = (bf16[128,2048]{1,0:T(8,128)(2,1)S(1)}, bf16[128,2048]{1,0:T(8,128)(2,1)S(1)}, u32[]{:S(2)}, u32[]{:S(2)}) collective-permute-start(bf16[128,2048]{1,0:T(8,128)(2,1)S(1)} %get-tuple-element.16), channel_id=1, source_target_pairs={{0,1},{1,0},{2,3},{3,2},{4,5},{5,4},{6,7},{7,6},{8,9},{9,8},{10,11... | collective-permute-start | bytes 1572872 | tf_op jit(solution)/shard_map/ppermute | solution.py:196
  25.6 31.5 %copy-start.9 = (s32[128,4]{0,1:T(4,128)S(1)}, s32[128,4]{0,1:T(4,128)}, u32[]{:S(2)}) copy-start(s32[128,4]{0,1:T(4,128)} %param.9) | copy-start | bytes 6148
  25.6 34.8 %copy-start.10 = (f32[128,4]{0,1:T(4,128)S(1)}, f32[128,4]{0,1:T(4,128)}, u32[]{:S(2)}) copy-start(f32[128,4]{0,1:T(4,128)} %param.10) | copy-start | bytes 6148
  25.7 15.0 %collective-permute-start = (bf16[128,2048]{1,0:T(8,128)(2,1)S(1)}, bf16[128,2048]{1,0:T(8,128)(2,1)S(1)}, u32[]{:S(2)}, u32[]{:S(2)}) collective-permute-start(bf16[128,2048]{1,0:T(8,128)(2,1)S(1)} %get-tuple-element.17.a_ref), channel_id=1, source_target_pairs={{0,4},{4,0},{8,12},{12,8},{16,20},{20,16},{24,28},{28,24},{32,36},... | collective-permute-start | bytes 1572872 | tf_op jit(solution)/shard_map/ppermute | solution.py:193
  36.9 5.2 %collective-permute-start.2 = (bf16[128,2048]{1,0:T(8,128)(2,1)S(1)}, bf16[128,2048]{1,0:T(8,128)(2,1)S(1)}, u32[]{:S(2)}, u32[]{:S(2)}) collective-permute-start(bf16[128,2048]{1,0:T(8,128)(2,1)S(1)} %collective-permute-done.1.c_ref), channel_id=1, source_target_pairs={{0,4},{4,0},{8,12},{12,8},{16,20},{20,16},{24,28},{28,24},{32,36},... | collective-permute-start | bytes 1572872 | tf_op jit(solution)/shard_map/ppermute | solution.py:193
  54.0 6.7 %collective-permute-start.3 = (bf16[256,256]{1,0:T(8,128)(2,1)S(1)}, bf16[256,256]{1,0:T(8,128)(2,1)S(1)}, u32[]{:S(2)}, u32[]{:S(2)}) collective-permute-start(bf16[256,256]{1,0:T(8,128)(2,1)S(1)} %get-tuple-element.10), channel_id=1, source_target_pairs={{0,1},{1,0},{2,3},{3,2},{4,5},{5,4},{6,7},{7,6},{8,9},{9,8},{10,11... | collective-permute-start | bytes 393224 | tf_op jit(solution)/shard_map/ppermute | solution.py:196
  57.2 3.3 %collective-permute-start.4 = (s32[4,128]{1,0:T(4,128)S(1)}, s32[4,128]{1,0:T(4,128)S(1)}, u32[]{:S(2)}, u32[]{:S(2)}) collective-permute-start(s32[4,128]{1,0:T(4,128)S(1)} %bitcast.19), channel_id=1, source_target_pairs={{0,4},{4,0},{8,12},{12,8},{16,20},{20,16},{24,28},{28,24},{32,36},... | collective-permute-start | bytes 6152 | tf_op jit(solution)/shard_map/ppermute | solution.py:193
  62.6 48.3 %copy-start.7 = (bf16[1,512,1408]{2,1,0:T(8,128)(2,1)S(1)}, bf16[1,512,1408]{2,1,0:T(8,128)(2,1)}, u32[]{:S(2)}) copy-start(bf16[1,512,1408]{2,1,0:T(8,128)(2,1)} %param.13) | copy-start | bytes 4325380
  62.6 48.2 %copy-start.8 = (bf16[1,1408,512]{2,1,0:T(8,128)(2,1)S(1)}, bf16[1,1408,512]{2,1,0:T(8,128)(2,1)}, u32[]{:S(2)}) copy-start(bf16[1,1408,512]{2,1,0:T(8,128)(2,1)} %param.14) | copy-start | bytes 4325380
  119.3 1.2 copy-start.4
  120.5 48.8 %all-to-all-start.2 = ((bf16[128,48,128]{2,1,0:T(8,128)(2,1)}), bf16[128,48,128]{2,1,0:T(8,128)(2,1)S(1)}, u32[]{:S(2)}, u32[]{:S(2)}) async-start(bf16[128,48,128]{2,1,0:T(8,128)(2,1)} %bitcast.14), calls=%async_computation.2 | async-start | bytes 3145728 | tf_op jit(solution)/shard_map/all_to_all | solution.py:199
  128.0 25.7 %collective-permute-start.6 = (bf16[128,32,128]{2,1,0:T(8,128)(2,1)S(1)}, bf16[128,32,128]{2,1,0:T(8,128)(2,1)S(1)}, u32[]{:S(2)}, u32[]{:S(2)}) collective-permute-start(bf16[128,32,128]{2,1,0:T(8,128)(2,1)S(1)} %all-to-all-done.w_ref.same_ref), channel_id=1, source_target_pairs={{0,1},{1,0},{2,3},{3,2},{4,5},{5,4},{6,7},{7,6},{8,9},{9,8},{10,11... | collective-permute-start | bytes 3145736 | tf_op jit(solution)/shard_map/ppermute | solution.py:196
  131.1 26.5 %collective-permute-start.5 = (bf16[128,32,128]{2,1,0:T(8,128)(2,1)S(1)}, bf16[128,32,128]{2,1,0:T(8,128)(2,1)S(1)}, u32[]{:S(2)}, u32[]{:S(2)}) collective-permute-start(bf16[128,32,128]{2,1,0:T(8,128)(2,1)S(1)} %all-to-all-done.w_ref.same_ref), channel_id=1, source_target_pairs={{0,4},{4,0},{8,12},{12,8},{16,20},{20,16},{24,28},{28,24},{32,36},... | collective-permute-start | bytes 3145736 | tf_op jit(solution)/shard_map/ppermute | solution.py:193
  153.7 6.0 %collective-permute-start.7 = (bf16[128,32,128]{2,1,0:T(8,128)(2,1)S(1)}, bf16[128,32,128]{2,1,0:T(8,128)(2,1)S(1)}, u32[]{:S(2)}, u32[]{:S(2)}) collective-permute-start(bf16[128,32,128]{2,1,0:T(8,128)(2,1)S(1)} %collective-permute-done.6.plane_ref), channel_id=1, source_target_pairs={{0,4},{4,0},{8,12},{12,8},{16,20},{20,16},{24,28},{28,24},{32,36},... | collective-permute-start | bytes 3145736 | tf_op jit(solution)/shard_map/ppermute | solution.py:193
  161.8 1.3 copy-start
  163.1 1.3 copy-start.2
  169.2 1.6 copy-start.1
  170.8 1.6 copy-start.3

commit v3 on v2

--- a/solution.py
+++ b/solution.py
@@ -8,6 +8,7 @@
 from jax.sharding import PartitionSpec as P
 
 SLOTS = 6
+PITCH = 136
 LANES = 128
 MIB = 2**20
 
@@ -22,12 +23,14 @@
     )
 
 
-def vmem_call(body, out_shape, scratch, limit_mib, flops, moved, arrays, scalars=0):
+def vmem_call(body, out_shape, scratch, limit_mib, flops, moved, arrays, scalars=0, far=0, far_out=False):
     return pl.pallas_call(
         body,
         out_shape=out_shape,
         in_specs=[pl.BlockSpec(memory_space=pltpu.SMEM)] * scalars
-        + [pl.BlockSpec(memory_space=pltpu.VMEM)] * arrays,
+        + [pl.BlockSpec(memory_space=pltpu.VMEM)] * arrays
+        + [pl.BlockSpec(memory_space=pl.ANY)] * far,
+        **({"out_specs": pl.BlockSpec(memory_space=pltpu.HBM)} if far_out else {}),
         scratch_shapes=scratch,
         compiler_params=pltpu.CompilerParams(vmem_limit_bytes=limit_mib * MIB),
         cost_estimate=pl.CostEstimate(flops=flops, bytes_accessed=moved, transcendentals=0),
@@ -61,13 +64,29 @@
                 low_ref[:, at] = (gate - high.astype(jnp.float32)).astype(jnp.bfloat16)
 
 
-def cast_kernel(plane_ref, down_ref, up_ref, out_ref):
-    shard = jnp.where(plane_ref[0] == 0, down_ref[...], up_ref[...])
+def cast_kernel(plane_ref, down_ref, up_ref, out_ref, shard, piece, in_sem, out_sem):
+    @pl.when(plane_ref[0] == 0)
+    def _():
+        pltpu.make_async_copy(down_ref, shard, in_sem).start()
+
+    @pl.when(plane_ref[0] != 0)
+    def _():
+        pltpu.make_async_copy(up_ref, shard, in_sem).start()
+
+    pltpu.make_async_copy(down_ref, shard, in_sem).wait()
     rows, width = shard.shape
     for j in range(width // LANES):
-        piece = shard[:, j * LANES : (j + 1) * LANES]
-        at = pl.ds(j * rows, rows)
-        out_ref[:, at, :] = jnp.broadcast_to(piece[None], (out_ref.shape[0], rows, LANES))
+        chunk = shard[:, j * LANES : (j + 1) * LANES]
+        piece[:, pl.ds(j * rows, rows), :] = jnp.broadcast_to(chunk[None], (piece.shape[0], rows, LANES))
+    count = piece.shape[0]
+    copies = [
+        pltpu.make_async_copy(piece, out_ref.at[pl.ds(n * count, count)], out_sem.at[n])
+        for n in range(out_ref.shape[0] // count)
+    ]
+    for copy in copies:
+        copy.start()
+    for copy in copies:
+        copy.wait()
 
 
 def half_weight(w_ref):
@@ -101,12 +120,13 @@
         for s in range(SLOTS):
             rows = dot(place_ref[half * SLOTS + s], both[half * tok : (half + 1) * tok])
             for j in range(chunks):
-                first = (half * SLOTS + s) * chunks + j
-                scr[pl.ds(first, experts, stride=block), :] = rows[:, j * LANES : (j + 1) * LANES]
-    out_ref[...] = scr[...].astype(jnp.bfloat16)
-
-
-def expert_kernel(chips, in_ref, up_ref, down_ref, out_ref, scr, lat, grad):
+                first = ((half * SLOTS + s) * chunks + j) * PITCH
+                scr[pl.ds(first, experts), :] = rows[:, j * LANES : (j + 1) * LANES]
+    for e in range(experts):
+        out_ref[pl.ds(e * block, block), :] = scr[pl.ds(e, block, stride=PITCH), :].astype(jnp.bfloat16)
+
+
+def expert_kernel(chips, in_ref, up_ref, down_ref, out_ref, scr, lat, grad, made, done, sems):
     width = lat.shape[1]
     chunks = width // LANES
     block = 2 * SLOTS * chunks
@@ -121,9 +141,10 @@
                 lat[at] = scr[pl.ds(first, chips, stride=2 * block), :].astype(jnp.bfloat16)
                 first += chunks // 2
                 grad[at] = scr[pl.ds(first, chips, stride=2 * block), :].astype(jnp.bfloat16)
-    per = lat.shape[0] // 3
+    tiles = 2
+    per = lat.shape[0] // tiles
     slots_per = per // chips
-    for m in range(3):
+    for m in range(tiles):
         at = pl.ds(m * per, per)
         act = jnp.maximum(dot(lat[at, :], up_ref[...]), 0.0)
         squared = jnp.square(act).astype(jnp.bfloat16)
@@ -135,32 +156,26 @@
             core, s = divmod(m * slots_per + q, SLOTS)
             for j in range(chunks):
                 part = (slice(q * chips, (q + 1) * chips), slice(j * LANES, (j + 1) * LANES))
-                first = core * block + s * chunks + j
-                scr[pl.ds(first, chips, stride=2 * block), :] = out[part]
-                scr[pl.ds(first + block // 2, chips, stride=2 * block), :] = back[part]
-    out_ref[...] = scr[...].astype(jnp.bfloat16)
-
-
-def weight_kernel(place_ref, same_ref, next_ref, plane_ref, far_ref, down_ref, up_ref):
-    first_plane, first_core = place_ref[0] == 0, place_ref[1] == 0
-    half = down_ref.shape[1] // 2
-    per = 16
-    for j in range(half // LANES):
-        rows = slice(j * per, (j + 1) * per)
-
-        def piece(ref):
-            return ref[:, rows, :].reshape(-1, LANES)
-
-        same, beside, plane, far = piece(same_ref), piece(next_ref), piece(plane_ref), piece(far_ref)
-        for low in range(2):
-            mine = jnp.where(first_core, (same, beside)[low], (beside, same)[low])
-            theirs = jnp.where(first_core, (plane, far)[low], (far, plane)[low])
-            at = pl.ds(low * half + j * LANES, LANES)
-            down_ref[:, at] = jnp.where(first_plane, mine, theirs)
-            up_ref[:, at] = jnp.where(first_plane, theirs, mine)
-
-
-def finish_kernel(experts, in_ref, high_ref, low_ref, down_ref, up_ref, layer_ref, grad_ref, scr, rows):
+                first = (s * chunks + j) * PITCH + core * chips
+                made[pl.ds(first, chips), :] = out[part]
+                made[pl.ds(first + block // 2 * PITCH, chips), :] = back[part]
+    parts = sems.shape[0]
+    copies = []
+    for n in range(parts):
+        for chip in range(n * chips // parts, (n + 1) * chips // parts):
+            for core in range(2):
+                rows = made[pl.ds(core * chips + chip, block, stride=PITCH), :]
+                done[pl.ds((2 * chip + core) * block, block), :] = rows.astype(jnp.bfloat16)
+        at = pl.ds(n * (2 * chips * block // parts), 2 * chips * block // parts)
+        copies.append(pltpu.make_async_copy(done.at[at], out_ref.at[at], sems.at[n]))
+        copies[-1].start()
+    for copy in copies:
+        copy.wait()
+
+
+def finish_kernel(
+    experts, place_ref, in_ref, high_ref, low_ref, same_ref, next_ref, plane_ref, far_ref, layer_ref, grad_ref, scr, rows
+):
     chunks = rows.shape[1] // (2 * LANES)
     block = 2 * SLOTS * chunks
     scr[...] = in_ref[...].astype(jnp.float32)
@@ -172,9 +187,26 @@
                 rows[at] = scr[pl.ds(first, experts, stride=block), :].astype(jnp.bfloat16)
     total = dot(high_ref[...], rows[...]) + dot(low_ref[...], rows[...])
     total = total.astype(jnp.bfloat16)
-    width = chunks * LANES
-    layer_ref[...] = contract_last(total[:, :width], up_ref[...]).astype(jnp.bfloat16)
-    grad_ref[...] = contract_last(total[:, width:], down_ref[...]).astype(jnp.bfloat16)
+    first_plane, first_core = place_ref[0] == 0, place_ref[1] == 0
+    half = chunks * LANES // 2
+
+    def swapped(yes, x):
+        return jnp.concatenate(
+            [jnp.where(yes, x[:, :half], x[:, half:]), jnp.where(yes, x[:, half:], x[:, :half])], axis=1
+        )
+
+    combined = swapped(first_core, total[:, : 2 * half])
+    grad_sum = swapped(first_core, total[:, 2 * half :])
+    mine = jnp.where(first_plane, grad_sum, combined)
+    theirs = jnp.where(first_plane, combined, grad_sum)
+
+    def project(x, this, that):
+        return contract_last(x, jnp.concatenate([half_weight(this), half_weight(that)], axis=1))
+
+    mine = project(mine, same_ref, next_ref)
+    theirs = project(theirs, plane_ref, far_ref)
+    layer_ref[...] = jnp.where(first_plane, theirs, mine).astype(jnp.bfloat16)
+    grad_ref[...] = jnp.where(first_plane, mine, theirs).astype(jnp.bfloat16)
 
 
 def on_device(tokens, expert_ids, gate_values, latent_down, latent_up, expert_up, expert_down, grad_out):
@@ -201,12 +233,19 @@
     cast = vmem_call(
         cast_kernel,
         jax.ShapeDtypeStruct((ep // 2, chunks * shard, LANES), bf16),
-        [],
-        8,
+        [
+            pltpu.VMEM((shard, width), bf16),
+            pltpu.VMEM((ep // 8, chunks * shard, LANES), bf16),
+            pltpu.SemaphoreType.DMA,
+            pltpu.SemaphoreType.DMA((4,)),
+        ],
+        61,
         0,
         MIB,
+        arrays=0,
         scalars=1,
-        arrays=2,
+        far=2,
+        far_out=True,
     )(place_of, latent_down, latent_up.T)
     same = exchange(cast.reshape(ep, chunks // 2 * shard, LANES))
 
@@ -243,7 +282,7 @@
     outbound = vmem_call(
         functools.partial(send_kernel, ep),
         jax.ShapeDtypeStruct((ep * block, LANES), bf16),
-        [pltpu.VMEM((ep * block, LANES), f32)],
+        [pltpu.VMEM((block * PITCH, LANES), f32)],
         12,
         4 * SLOTS * tok * ep * width,
         3 * MIB,
@@ -262,18 +301,18 @@
             pltpu.VMEM((ep * block, LANES), f32),
             pltpu.VMEM((rows, width), bf16),
             pltpu.VMEM((rows, width), bf16),
+            pltpu.VMEM((block * PITCH, LANES), f32),
+            pltpu.VMEM((ep * block, LANES), bf16),
+            pltpu.SemaphoreType.DMA((4,)),
         ],
-        32,
+        36,
         8 * rows * width * hidden,
         8 * MIB,
         arrays=3,
+        far_out=True,
     )(arrived.reshape(ep * block, LANES), expert_up[0], expert_down[0])
 
     returned = exchange(done.reshape(ep, block, LANES))
-    whole = jax.ShapeDtypeStruct((wide, width), bf16)
-    down, up = vmem_call(
-        weight_kernel, (whole, whole), [], 16, 0, 8 * MIB, scalars=1, arrays=4
-    )(place_of, same, beside(same), other, beside(other))
     result = jax.ShapeDtypeStruct((tok, wide), bf16)
     return vmem_call(
         functools.partial(finish_kernel, ep),
@@ -282,11 +321,12 @@
             pltpu.VMEM((ep * block, LANES), f32),
             pltpu.VMEM((SLOTS * ep, 2 * width), bf16),
         ],
-        20,
+        51,
         4 * tok * wide * width,
         7 * MIB,
-        arrays=5,
-    )(returned.reshape(ep * block, LANES), high, low, down, up)
+        arrays=7,
+        scalars=1,
+    )(place_of, returned.reshape(ep * block, LANES), high, low, same, beside(same), other, beside(other))
 
 
 def solution(mesh):

time: 178 us -> 175 us (0.983)
  local copies, waits for them, and re-layouts: 8.46 us -> 0.04 us
  waiting for transfers between devices: 48 us -> 52.6 us
    unnamed x26 -> x16, local copies, waits for them, and re-layouts: 8.46 us -> 0.04 us
    all_to_all x2, waiting for transfers between devices: 16 us -> 20.3 us  [exchange(): return lax.all_to_all(x, 'ep', split_axis=0, concat_axis=0, tiled=True)]
    pallas_call x1, Pallas kernels: 3.98 us -> 6.27 us  [on_device(): vmem_call(functools.partial(finish_kernel, ep), (result, result), [pltpu....]
    pallas_call x1 -> x0, Pallas kernels: 2.11 us -> none  [on_device(): vmem_call(weight_kernel, (whole, whole), [], 16, 0, 8 * MIB, scalars=1, a...]
  transfers between devices with their start and end apart: 10 -> 10, of which waited for: 7 -> 7; matrix products, arithmetic and copies ran while one was open for 0% -> 0% of each run, Pallas kernels for 1% -> 0%
where the time goes in v3:
time: 175 us; the launch traced here: 174 us
  waiting for transfers between devices  52.6 us (30%)
  starting transfers between devices  51.8 us (30%)
  blocking collectives  48.2 us (28%)
  Pallas kernels  19.6 us (11%)
    all_to_all x1, blocking collectives, exchange(): return lax.all_to_all(x, 'ep', split_axis=0, concat_axis=0, tiled=True)  48.2 us
    ppermute x3, waiting for transfers between devices, next_plane(): return lax.ppermute(x, 'dp', [(i, i ^ 1) for i in range(dp)])  27.6 us
    all_to_all x2, starting transfers between devices, exchange(): return lax.all_to_all(x, 'ep', split_axis=0, concat_axis=0, tiled=True)  26.4 us
    all_to_all x2, waiting for transfers between devices, exchange(): return lax.all_to_all(x, 'ep', split_axis=0, concat_axis=0, tiled=True)  20.3 us
    ppermute x5, starting transfers between devices, beside(): return lax.ppermute(x, 'ep', [(i, i ^ 1) for i in range(ep)])  16.1 us
    ppermute x3, starting transfers between devices, next_plane(): return lax.ppermute(x, 'dp', [(i, i ^ 1) for i in range(dp)])  9.36 us
    pallas_call x1, Pallas kernels, on_device(): vmem_call(functools.partial(expert_kernel, ep // 2), jax.ShapeDtypeStruct...  8.22 us
    pallas_call x1, Pallas kernels, on_device(): vmem_call(functools.partial(finish_kernel, ep), (result, result), [pltpu....  6.27 us
  transfers between devices with their start and end apart: 10, of which 7 were waited for; matrix products, arithmetic and copies ran while one was open for 0% of the time, Pallas kernels for 0%

profile of v3, /device:TPU:1, one launch (start us, length us, event | category | flops | bytes accessed | tf_op | source)
XLA Modules:
  0.0 173.9 jit_solution(417574145710005126)
XLA Ops:
  0.6 0.6 pad_add_fusion.plane_ref.place_ref
  1.3 2.6 %shard_map.95 = bf16[64,64,128]{2,1,0:T(8,128)(2,1)} custom-call(s32[2]{0:T(128)} %pad_add_fusion.plane_ref.place_ref, bf16[16,512]{1,0:T(8,128)(2,1)} %down_ref.1, bf16[16,512]{1,0:T(8,128)(2,1)} %bitcast.20), custom_call_target="tpu_custom_call" | custom-call | bytes 1048576 | tf_op jit(solution)/shard_map/pallas_call | solution.py:233
  3.9 18.4 %all-to-all-start = ((bf16[128,32,128]{2,1,0:T(8,128)(2,1)}), bf16[128,32,128]{2,1,0:T(8,128)(2,1)S(1)}, u32[]{:S(2)}, u32[]{:S(2)}) async-start(bf16[128,32,128]{2,1,0:T(8,128)(2,1)} %bitcast.19), calls=%async_computation | async-start | bytes 2097152 | tf_op jit(solution)/shard_map/all_to_all | solution.py:231
  22.5 3.1 %collective-permute-start.1 = (bf16[128,2048]{1,0:T(8,128)(2,1)S(1)}, bf16[128,2048]{1,0:T(8,128)(2,1)S(1)}, u32[]{:S(2)}, u32[]{:S(2)}) collective-permute-start(bf16[128,2048]{1,0:T(8,128)(2,1)S(1)} %get-tuple-element.12), channel_id=1, source_target_pairs={{0,1},{1,0},{2,3},{3,2},{4,5},{5,4},{6,7},{7,6},{8,9},{9,8},{10,11... | collective-permute-start | bytes 1572872 | tf_op jit(solution)/shard_map/ppermute | solution.py:228
  25.6 3.1 %collective-permute-start = (bf16[128,2048]{1,0:T(8,128)(2,1)S(1)}, bf16[128,2048]{1,0:T(8,128)(2,1)S(1)}, u32[]{:S(2)}, u32[]{:S(2)}) collective-permute-start(bf16[128,2048]{1,0:T(8,128)(2,1)S(1)} %get-tuple-element.13.a_ref), channel_id=1, source_target_pairs={{0,4},{4,0},{8,12},{12,8},{16,20},{20,16},{24,28},{28,24},{32,36},... | collective-permute-start | bytes 1572872 | tf_op jit(solution)/shard_map/ppermute | solution.py:225
  28.7 8.2 %collective-permute-done.1.c_ref = bf16[128,2048]{1,0:T(8,128)(2,1)S(1)} collective-permute-done((bf16[128,2048]{1,0:T(8,128)(2,1)S(1)}, bf16[128,2048]{1,0:T(8,128)(2,1)S(1)}, u32[]{:S(2)}, u32[]{:S(2)}) %collective-permute-start.1) | collective-permute-done | bytes 524320 | tf_op jit(solution)/shard_map/ppermute | solution.py:228
  36.9 3.7 %collective-permute-start.2 = (bf16[128,2048]{1,0:T(8,128)(2,1)S(1)}, bf16[128,2048]{1,0:T(8,128)(2,1)S(1)}, u32[]{:S(2)}, u32[]{:S(2)}) collective-permute-start(bf16[128,2048]{1,0:T(8,128)(2,1)S(1)} %collective-permute-done.1.c_ref), channel_id=1, source_target_pairs={{0,4},{4,0},{8,12},{12,8},{16,20},{20,16},{24,28},{28,24},{32,36},... | collective-permute-start | bytes 1572872 | tf_op jit(solution)/shard_map/ppermute | solution.py:225
  40.6 1.5 collective-permute-done.2.d_ref
  42.1 11.1 %all-to-all-done.w_ref.same_ref = bf16[128,32,128]{2,1,0:T(8,128)(2,1)S(1)} async-done(((bf16[128,32,128]{2,1,0:T(8,128)(2,1)}), bf16[128,32,128]{2,1,0:T(8,128)(2,1)S(1)}, u32[]{:S(2)}, u32[]{:S(2)}) %all-to-all-start) | async-done | bytes 1048608 | tf_op jit(solution)/shard_map/all_to_all | solution.py:231
  53.3 0.7 shard_map.96
  54.0 3.1 %collective-permute-start.3 = (bf16[256,256]{1,0:T(8,128)(2,1)S(1)}, bf16[256,256]{1,0:T(8,128)(2,1)S(1)}, u32[]{:S(2)}, u32[]{:S(2)}) collective-permute-start(bf16[256,256]{1,0:T(8,128)(2,1)S(1)} %get-tuple-element.8), channel_id=1, source_target_pairs={{0,1},{1,0},{2,3},{3,2},{4,5},{5,4},{6,7},{7,6},{8,9},{9,8},{10,11... | collective-permute-start | bytes 393224 | tf_op jit(solution)/shard_map/ppermute | solution.py:228
  57.1 2.5 %collective-permute-start.4 = (s32[4,128]{1,0:T(4,128)S(1)}, s32[4,128]{1,0:T(4,128)S(1)}, u32[]{:S(2)}, u32[]{:S(2)}) collective-permute-start(s32[4,128]{1,0:T(4,128)S(1)} %bitcast.16), channel_id=1, source_target_pairs={{0,4},{4,0},{8,12},{12,8},{16,20},{20,16},{24,28},{28,24},{32,36},... | collective-permute-start | bytes 6152 | tf_op jit(solution)/shard_map/ppermute | solution.py:225
  59.6 0.8 collective-permute-done.4.other_ids
  60.8 1.5 shard_map.98
  62.3 48.2 %all_to_all.15 = bf16[128,48,128]{2,1,0:T(8,128)(2,1)S(1)} all-to-all(bf16[128,48,128]{2,1,0:T(8,128)(2,1)S(1)} %bitcast.12), channel_id=1, replica_groups=mesh['ep'=128,'dp'=4] {'ep'}, dimensions={0} | all-to-all | bytes 3145728 | tf_op jit(solution)/shard_map/all_to_all | solution.py:231
  110.5 8.2 %shard_map.99 = bf16[6144,128]{1,0:T(8,128)(2,1)} custom-call(bf16[6144,128]{1,0:T(8,128)(2,1)S(1)} %bitcast.13, bf16[512,1408]{1,0:T(8,128)(2,1)S(1)} %bitcast.14, bf16[1408,512]{1,0:T(8,128)(2,1)S(1)} %bitcast.15), custom_call_target="tpu_custom_call" | custom-call | flops 4429185024 | bytes 8388608 | tf_op jit(solution)/shard_map/pallas_call | solution.py:297
  118.7 8.0 %all-to-all-start.2 = ((bf16[128,48,128]{2,1,0:T(8,128)(2,1)}), bf16[128,48,128]{2,1,0:T(8,128)(2,1)}, u32[]{:S(2)}, u32[]{:S(2)}) async-start(bf16[128,48,128]{2,1,0:T(8,128)(2,1)} %bitcast.10), calls=%async_computation.2 | async-start | bytes 3145728 | tf_op jit(solution)/shard_map/all_to_all | solution.py:231
  126.7 3.1 %collective-permute-start.6 = (bf16[128,32,128]{2,1,0:T(8,128)(2,1)S(1)}, bf16[128,32,128]{2,1,0:T(8,128)(2,1)S(1)}, u32[]{:S(2)}, u32[]{:S(2)}) collective-permute-start(bf16[128,32,128]{2,1,0:T(8,128)(2,1)S(1)} %all-to-all-done.w_ref.same_ref), channel_id=1, source_target_pairs={{0,1},{1,0},{2,3},{3,2},{4,5},{5,4},{6,7},{7,6},{8,9},{9,8},{10,11... | collective-permute-start | bytes 3145736 | tf_op jit(solution)/shard_map/ppermute | solution.py:228
  129.8 3.1 %collective-permute-start.5 = (bf16[128,32,128]{2,1,0:T(8,128)(2,1)S(1)}, bf16[128,32,128]{2,1,0:T(8,128)(2,1)S(1)}, u32[]{:S(2)}, u32[]{:S(2)}) collective-permute-start(bf16[128,32,128]{2,1,0:T(8,128)(2,1)S(1)} %all-to-all-done.w_ref.same_ref), channel_id=1, source_target_pairs={{0,4},{4,0},{8,12},{12,8},{16,20},{20,16},{24,28},{28,24},{32,36},... | collective-permute-start | bytes 3145736 | tf_op jit(solution)/shard_map/ppermute | solution.py:225
  133.0 19.4 %collective-permute-done.6.plane_ref = bf16[128,32,128]{2,1,0:T(8,128)(2,1)S(1)} collective-permute-done((bf16[128,32,128]{2,1,0:T(8,128)(2,1)S(1)}, bf16[128,32,128]{2,1,0:T(8,128)(2,1)S(1)}, u32[]{:S(2)}, u32[]{:S(2)}) %collective-permute-start.6) | collective-permute-done | bytes 1048608 | tf_op jit(solution)/shard_map/ppermute | solution.py:228
  152.4 3.7 %collective-permute-start.7 = (bf16[128,32,128]{2,1,0:T(8,128)(2,1)S(1)}, bf16[128,32,128]{2,1,0:T(8,128)(2,1)}, u32[]{:S(2)}, u32[]{:S(2)}) collective-permute-start(bf16[128,32,128]{2,1,0:T(8,128)(2,1)S(1)} %collective-permute-done.6.plane_ref), channel_id=1, source_target_pairs={{0,4},{4,0},{8,12},{12,8},{16,20},{20,16},{24,28},{28,24},{32,36},... | collective-permute-start | bytes 3145736 | tf_op jit(solution)/shard_map/ppermute | solution.py:225
  156.1 2.4 %collective-permute-done.7.far_ref = bf16[128,32,128]{2,1,0:T(8,128)(2,1)} collective-permute-done((bf16[128,32,128]{2,1,0:T(8,128)(2,1)S(1)}, bf16[128,32,128]{2,1,0:T(8,128)(2,1)}, u32[]{:S(2)}, u32[]{:S(2)}) %collective-permute-start.7) | collective-permute-done | bytes 1048608 | tf_op jit(solution)/shard_map/ppermute | solution.py:225
  158.5 9.2 %all-to-all-done.2 = bf16[128,48,128]{2,1,0:T(8,128)(2,1)} async-done(((bf16[128,48,128]{2,1,0:T(8,128)(2,1)}), bf16[128,48,128]{2,1,0:T(8,128)(2,1)}, u32[]{:S(2)}, u32[]{:S(2)}) %all-to-all-start.2) | async-done | bytes 1572896 | tf_op jit(solution)/shard_map/all_to_all | solution.py:231
  167.6 6.3 %shard_map.100 = (bf16[128,2048]{1,0:T(8,128)(2,1)}, bf16[128,2048]{1,0:T(8,128)(2,1)}) custom-call(s32[2]{0:T(128)S(1)} %copy-done, bf16[6144,128]{1,0:T(8,128)(2,1)} %bitcast.11.in_ref, bf16[128,768]{1,0:T(8,128)(2,1)S(1)} %get-tuple-element.10.high_ref, bf16[128,768]{1,0:T(8,128)(2,1)S(1)} %get-tuple-element.11.low_ref, ...), custom_call_target="tpu_custom_call" | custom-call | flops 536870912 | bytes 7340032 | tf_op jit(solution)/shard_map/pallas_call | solution.py:317
  (21 shorter events, 0.4 us)
Async XLA Ops:
  1.3 21.1 %copy-start.6 = (bf16[128,2048]{1,0:T(8,128)(2,1)S(1)}, bf16[128,2048]{1,0:T(8,128)(2,1)}, u32[]{:S(2)}) copy-start(bf16[128,2048]{1,0:T(8,128)(2,1)} %param.15) | copy-start | bytes 1572868
  1.3 21.1 %copy-start.7 = (bf16[128,2048]{1,0:T(8,128)(2,1)S(1)}, bf16[128,2048]{1,0:T(8,128)(2,1)}, u32[]{:S(2)}) copy-start(bf16[128,2048]{1,0:T(8,128)(2,1)} %param.8) | copy-start | bytes 1572868
  3.9 49.3 %all-to-all-start = ((bf16[128,32,128]{2,1,0:T(8,128)(2,1)}), bf16[128,32,128]{2,1,0:T(8,128)(2,1)S(1)}, u32[]{:S(2)}, u32[]{:S(2)}) async-start(bf16[128,32,128]{2,1,0:T(8,128)(2,1)} %bitcast.19), calls=%async_computation | async-start | bytes 2097152 | tf_op jit(solution)/shard_map/all_to_all | solution.py:231
  22.5 14.4 %collective-permute-start.1 = (bf16[128,2048]{1,0:T(8,128)(2,1)S(1)}, bf16[128,2048]{1,0:T(8,128)(2,1)S(1)}, u32[]{:S(2)}, u32[]{:S(2)}) collective-permute-start(bf16[128,2048]{1,0:T(8,128)(2,1)S(1)} %get-tuple-element.12), channel_id=1, source_target_pairs={{0,1},{1,0},{2,3},{3,2},{4,5},{5,4},{6,7},{7,6},{8,9},{9,8},{10,11... | collective-permute-start | bytes 1572872 | tf_op jit(solution)/shard_map/ppermute | solution.py:228
  25.6 31.5 %copy-start.3 = (s32[128,4]{0,1:T(4,128)S(1)}, s32[128,4]{0,1:T(4,128)}, u32[]{:S(2)}) copy-start(s32[128,4]{0,1:T(4,128)} %param.9) | copy-start | bytes 6148
  25.6 34.8 %copy-start.4 = (f32[128,4]{0,1:T(4,128)S(1)}, f32[128,4]{0,1:T(4,128)}, u32[]{:S(2)}) copy-start(f32[128,4]{0,1:T(4,128)} %param.10) | copy-start | bytes 6148
  25.6 35.1 %copy-start = (s32[2]{0:T(128)S(1)}, s32[2]{0:T(128)}, u32[]{:S(2)}) copy-start(s32[2]{0:T(128)} %pad_add_fusion.plane_ref.place_ref) | copy-start | bytes 28
  25.6 15.0 %collective-permute-start = (bf16[128,2048]{1,0:T(8,128)(2,1)S(1)}, bf16[128,2048]{1,0:T(8,128)(2,1)S(1)}, u32[]{:S(2)}, u32[]{:S(2)}) collective-permute-start(bf16[128,2048]{1,0:T(8,128)(2,1)S(1)} %get-tuple-element.13.a_ref), channel_id=1, source_target_pairs={{0,4},{4,0},{8,12},{12,8},{16,20},{20,16},{24,28},{28,24},{32,36},... | collective-permute-start | bytes 1572872 | tf_op jit(solution)/shard_map/ppermute | solution.py:225
  36.9 5.2 %collective-permute-start.2 = (bf16[128,2048]{1,0:T(8,128)(2,1)S(1)}, bf16[128,2048]{1,0:T(8,128)(2,1)S(1)}, u32[]{:S(2)}, u32[]{:S(2)}) collective-permute-start(bf16[128,2048]{1,0:T(8,128)(2,1)S(1)} %collective-permute-done.1.c_ref), channel_id=1, source_target_pairs={{0,4},{4,0},{8,12},{12,8},{16,20},{20,16},{24,28},{28,24},{32,36},... | collective-permute-start | bytes 1572872 | tf_op jit(solution)/shard_map/ppermute | solution.py:225
  54.0 6.7 %collective-permute-start.3 = (bf16[256,256]{1,0:T(8,128)(2,1)S(1)}, bf16[256,256]{1,0:T(8,128)(2,1)S(1)}, u32[]{:S(2)}, u32[]{:S(2)}) collective-permute-start(bf16[256,256]{1,0:T(8,128)(2,1)S(1)} %get-tuple-element.8), channel_id=1, source_target_pairs={{0,1},{1,0},{2,3},{3,2},{4,5},{5,4},{6,7},{7,6},{8,9},{9,8},{10,11... | collective-permute-start | bytes 393224 | tf_op jit(solution)/shard_map/ppermute | solution.py:228
  57.1 3.3 %collective-permute-start.4 = (s32[4,128]{1,0:T(4,128)S(1)}, s32[4,128]{1,0:T(4,128)S(1)}, u32[]{:S(2)}, u32[]{:S(2)}) collective-permute-start(s32[4,128]{1,0:T(4,128)S(1)} %bitcast.16), channel_id=1, source_target_pairs={{0,4},{4,0},{8,12},{12,8},{16,20},{20,16},{24,28},{28,24},{32,36},... | collective-permute-start | bytes 6152 | tf_op jit(solution)/shard_map/ppermute | solution.py:225
  62.3 48.3 %copy-start.1 = (bf16[1,512,1408]{2,1,0:T(8,128)(2,1)S(1)}, bf16[1,512,1408]{2,1,0:T(8,128)(2,1)}, u32[]{:S(2)}) copy-start(bf16[1,512,1408]{2,1,0:T(8,128)(2,1)} %param.13) | copy-start | bytes 4325380
  62.3 48.2 %copy-start.2 = (bf16[1,1408,512]{2,1,0:T(8,128)(2,1)S(1)}, bf16[1,1408,512]{2,1,0:T(8,128)(2,1)}, u32[]{:S(2)}) copy-start(bf16[1,1408,512]{2,1,0:T(8,128)(2,1)} %param.14) | copy-start | bytes 4325380
  118.7 48.9 %all-to-all-start.2 = ((bf16[128,48,128]{2,1,0:T(8,128)(2,1)}), bf16[128,48,128]{2,1,0:T(8,128)(2,1)}, u32[]{:S(2)}, u32[]{:S(2)}) async-start(bf16[128,48,128]{2,1,0:T(8,128)(2,1)} %bitcast.10), calls=%async_computation.2 | async-start | bytes 3145728 | tf_op jit(solution)/shard_map/all_to_all | solution.py:231
  126.7 25.7 %collective-permute-start.6 = (bf16[128,32,128]{2,1,0:T(8,128)(2,1)S(1)}, bf16[128,32,128]{2,1,0:T(8,128)(2,1)S(1)}, u32[]{:S(2)}, u32[]{:S(2)}) collective-permute-start(bf16[128,32,128]{2,1,0:T(8,128)(2,1)S(1)} %all-to-all-done.w_ref.same_ref), channel_id=1, source_target_pairs={{0,1},{1,0},{2,3},{3,2},{4,5},{5,4},{6,7},{7,6},{8,9},{9,8},{10,11... | collective-permute-start | bytes 3145736 | tf_op jit(solution)/shard_map/ppermute | solution.py:228
  129.8 26.3 %collective-permute-start.5 = (bf16[128,32,128]{2,1,0:T(8,128)(2,1)S(1)}, bf16[128,32,128]{2,1,0:T(8,128)(2,1)S(1)}, u32[]{:S(2)}, u32[]{:S(2)}) collective-permute-start(bf16[128,32,128]{2,1,0:T(8,128)(2,1)S(1)} %all-to-all-done.w_ref.same_ref), channel_id=1, source_target_pairs={{0,4},{4,0},{8,12},{12,8},{16,20},{20,16},{24,28},{28,24},{32,36},... | collective-permute-start | bytes 3145736 | tf_op jit(solution)/shard_map/ppermute | solution.py:225
  152.4 15.2 %copy-start.5 = (bf16[128,32,128]{2,1,0:T(8,128)(2,1)}, bf16[128,32,128]{2,1,0:T(8,128)(2,1)S(1)}, u32[]{:S(2)}) copy-start(bf16[128,32,128]{2,1,0:T(8,128)(2,1)S(1)} %collective-permute-done.6.plane_ref) | copy-start | bytes 3145732
  152.4 6.1 %collective-permute-start.7 = (bf16[128,32,128]{2,1,0:T(8,128)(2,1)S(1)}, bf16[128,32,128]{2,1,0:T(8,128)(2,1)}, u32[]{:S(2)}, u32[]{:S(2)}) collective-permute-start(bf16[128,32,128]{2,1,0:T(8,128)(2,1)S(1)} %collective-permute-done.6.plane_ref), channel_id=1, source_target_pairs={{0,4},{4,0},{8,12},{12,8},{16,20},{20,16},{24,28},{28,24},{32,36},... | collective-permute-start | bytes 3145736 | tf_op jit(solution)/shard_map/ppermute | solution.py:225

commit v4 on v3

--- a/solution.py
+++ b/solution.py
@@ -23,12 +23,11 @@
     )
 
 
-def vmem_call(body, out_shape, scratch, limit_mib, flops, moved, arrays, scalars=0, far=0, far_out=False):
+def vmem_call(body, out_shape, scratch, limit_mib, flops, moved, arrays, far=0, far_out=False):
     return pl.pallas_call(
         body,
         out_shape=out_shape,
-        in_specs=[pl.BlockSpec(memory_space=pltpu.SMEM)] * scalars
-        + [pl.BlockSpec(memory_space=pltpu.VMEM)] * arrays
+        in_specs=[pl.BlockSpec(memory_space=pltpu.VMEM)] * arrays
         + [pl.BlockSpec(memory_space=pl.ANY)] * far,
         **({"out_specs": pl.BlockSpec(memory_space=pltpu.HBM)} if far_out else {}),
         scratch_shapes=scratch,
@@ -64,12 +63,14 @@
                 low_ref[:, at] = (gate - high.astype(jnp.float32)).astype(jnp.bfloat16)
 
 
-def cast_kernel(plane_ref, down_ref, up_ref, out_ref, shard, piece, in_sem, out_sem):
-    @pl.when(plane_ref[0] == 0)
+def cast_kernel(down_ref, up_ref, out_ref, shard, piece, in_sem, out_sem):
+    first_plane = lax.axis_index("dp") % 2 == 0
+
+    @pl.when(first_plane)
     def _():
         pltpu.make_async_copy(down_ref, shard, in_sem).start()
 
-    @pl.when(plane_ref[0] != 0)
+    @pl.when(jnp.logical_not(first_plane))
     def _():
         pltpu.make_async_copy(up_ref, shard, in_sem).start()
 
@@ -107,8 +108,8 @@
         out_ref[pl.ds(n % 2 * tok, tok), :] = dot(x_ref[...], weight).astype(jnp.bfloat16)
 
 
-def send_kernel(experts, plane_ref, mine_ref, swapped_ref, place_ref, out_ref, scr):
-    first_plane = plane_ref[0] == 0
+def send_kernel(experts, mine_ref, swapped_ref, place_ref, out_ref, scr):
+    first_plane = lax.axis_index("dp") % 2 == 0
     mine, swapped = mine_ref[...], swapped_ref[...]
     latent = jnp.where(first_plane, mine, swapped)
     grad = jnp.where(first_plane, swapped, mine)
@@ -174,11 +175,21 @@
 
 
 def finish_kernel(
-    experts, place_ref, in_ref, high_ref, low_ref, same_ref, next_ref, plane_ref, far_ref, layer_ref, grad_ref, scr, rows
+    experts, high_ref, low_ref, same_ref, next_ref, plane_ref, far_ref, in_ref, layer_ref, grad_ref,
+    scr, rows, landed, sems,
 ):
     chunks = rows.shape[1] // (2 * LANES)
     block = 2 * SLOTS * chunks
-    scr[...] = in_ref[...].astype(jnp.float32)
+    per = in_ref.shape[0] // sems.shape[0]
+    pieces = [pl.ds(n * per, per) for n in range(sems.shape[0])]
+    copies = [
+        pltpu.make_async_copy(in_ref.at[at], landed.at[at], sems.at[n]) for n, at in enumerate(pieces)
+    ]
+    for copy in copies:
+        copy.start()
+    for copy, at in zip(copies, pieces):
+        copy.wait()
+        scr[at, :] = landed[at, :].astype(jnp.float32)
     for s in range(SLOTS):
         for kind in range(2):
             for j in range(chunks):
@@ -187,7 +198,7 @@
                 rows[at] = scr[pl.ds(first, experts, stride=block), :].astype(jnp.bfloat16)
     total = dot(high_ref[...], rows[...]) + dot(low_ref[...], rows[...])
     total = total.astype(jnp.bfloat16)
-    first_plane, first_core = place_ref[0] == 0, place_ref[1] == 0
+    first_plane, first_core = lax.axis_index("dp") % 2 == 0, lax.axis_index("ep") % 2 == 0
     half = chunks * LANES // 2
 
     def swapped(yes, x):
@@ -216,9 +227,6 @@
     hidden = expert_up.shape[2]
     chunks = width // LANES
     block = 2 * SLOTS * chunks
-    core = (lax.axis_index("ep") % 2).astype(jnp.int32)
-    plane = (lax.axis_index("dp") % 2).astype(jnp.int32)
-    place_of = jnp.stack([plane, core])
     bf16, f32 = jnp.bfloat16, jnp.float32
 
     def beside(x):
@@ -243,13 +251,12 @@
         0,
         MIB,
         arrays=0,
-        scalars=1,
         far=2,
         far_out=True,
-    )(place_of, latent_down, latent_up.T)
+    )(latent_down, latent_up.T)
     same = exchange(cast.reshape(ep, chunks // 2 * shard, LANES))
 
-    first_plane = plane == 0
+    first_plane = lax.axis_index("dp") % 2 == 0
     own = jnp.where(first_plane, tokens, grad_out)
     theirs = next_plane(jnp.where(first_plane, grad_out, tokens))
     own_ids = expert_ids.T
@@ -268,6 +275,7 @@
         arrays=3,
     )(own_ids, beside(own_ids), gate_values.T)
 
+    own_after, place, high, low = lax.optimization_barrier((own, place, high, low))
     projected = jax.ShapeDtypeStruct((2 * tok, width // 2), bf16)
     mine, away = vmem_call(
         project_kernel,
@@ -277,7 +285,7 @@
         4 * tok * wide * width,
         4 * MIB,
         arrays=5,
-    )(own, beside(own), theirs, beside(theirs), same)
+    )(own_after, beside(own), theirs, beside(theirs), same)
 
     outbound = vmem_call(
         functools.partial(send_kernel, ep),
@@ -286,9 +294,8 @@
         12,
         4 * SLOTS * tok * ep * width,
         3 * MIB,
-        scalars=1,
         arrays=3,
-    )(place_of, mine, next_plane(away), place)
+    )(mine, next_plane(away), place)
 
     arrived = exchange(outbound.reshape(ep, block, LANES))
     other = next_plane(same)
@@ -320,13 +327,15 @@
         [
             pltpu.VMEM((ep * block, LANES), f32),
             pltpu.VMEM((SLOTS * ep, 2 * width), bf16),
+            pltpu.VMEM((ep * block, LANES), bf16),
+            pltpu.SemaphoreType.DMA((4,)),
         ],
         51,
         4 * tok * wide * width,
         7 * MIB,
-        arrays=7,
-        scalars=1,
-    )(place_of, returned.reshape(ep * block, LANES), high, low, same, beside(same), other, beside(other))
+        arrays=6,
+        far=1,
+    )(high, low, same, beside(same), other, beside(other), returned.reshape(ep * block, LANES))
 
 
 def solution(mesh):

time: 175 us -> 174 us (level)
    ppermute x3, waiting for transfers between devices: 27.6 us -> 31.2 us  [next_plane(): return lax.ppermute(x, 'dp', [(i, i ^ 1) for i in range(dp)])]
    all_to_all x2, waiting for transfers between devices: 20.3 us -> 17 us  [exchange(): return lax.all_to_all(x, 'ep', split_axis=0, concat_axis=0, tiled=True)]
where the time goes in v4:
time: 174 us; the launch traced here: 173 us
  waiting for transfers between devices  51.8 us (30%)
  starting transfers between devices  51.4 us (30%)
  blocking collectives  48.3 us (28%)
  Pallas kernels  19.2 us (11%)
    all_to_all x1, blocking collectives, exchange(): return lax.all_to_all(x, 'ep', split_axis=0, concat_axis=0, tiled=True)  48.3 us
    ppermute x3, waiting for transfers between devices, next_plane(): return lax.ppermute(x, 'dp', [(i, i ^ 1) for i in range(dp)])  31.2 us
    all_to_all x2, starting transfers between devices, exchange(): return lax.all_to_all(x, 'ep', split_axis=0, concat_axis=0, tiled=True)  26.5 us
    all_to_all x2, waiting for transfers between devices, exchange(): return lax.all_to_all(x, 'ep', split_axis=0, concat_axis=0, tiled=True)  17 us
    ppermute x5, starting transfers between devices, beside(): return lax.ppermute(x, 'ep', [(i, i ^ 1) for i in range(ep)])  15.5 us
    ppermute x3, starting transfers between devices, next_plane(): return lax.ppermute(x, 'dp', [(i, i ^ 1) for i in range(dp)])  9.37 us
    pallas_call x1, Pallas kernels, on_device(): vmem_call(functools.partial(expert_kernel, ep // 2), jax.ShapeDtypeStruct...  8.22 us
    pallas_call x1, Pallas kernels, on_device(): vmem_call(functools.partial(finish_kernel, ep), (result, result), [pltpu....  7.07 us
  transfers between devices with their start and end apart: 10, of which 7 were waited for; matrix products, arithmetic and copies ran while one was open for 0% of the time, Pallas kernels for 0%

profile of v4, /device:TPU:1, one launch (start us, length us, event | category | flops | bytes accessed | tf_op | source)
XLA Modules:
  0.0 173.1 jit_solution(10316737774022455374)
XLA Ops:
  0.7 1.9 %shard_map.96 = bf16[64,64,128]{2,1,0:T(8,128)(2,1)} custom-call(bf16[16,512]{1,0:T(8,128)(2,1)} %down_ref.1, bf16[16,512]{1,0:T(8,128)(2,1)} %bitcast.18), custom_call_target="tpu_custom_call" | custom-call | bytes 1048576 | tf_op jit(solution)/shard_map/pallas_call | solution.py:241
  2.6 18.4 %all-to-all-start = ((bf16[128,32,128]{2,1,0:T(8,128)(2,1)}), bf16[128,32,128]{2,1,0:T(8,128)(2,1)S(1)}, u32[]{:S(2)}, u32[]{:S(2)}) async-start(bf16[128,32,128]{2,1,0:T(8,128)(2,1)} %bitcast.17), calls=%async_computation | async-start | bytes 2097152 | tf_op jit(solution)/shard_map/all_to_all | solution.py:239
  21.1 3.1 %collective-permute-start.5 = (bf16[128,2048]{1,0:T(8,128)(2,1)S(1)}, bf16[128,2048]{1,0:T(8,128)(2,1)S(1)}, u32[]{:S(2)}, u32[]{:S(2)}) collective-permute-start(bf16[128,2048]{1,0:T(8,128)(2,1)S(1)} %get-tuple-element.20), channel_id=1, source_target_pairs={{0,1},{1,0},{2,3},{3,2},{4,5},{5,4},{6,7},{7,6},{8,9},{9,8},{10,11... | collective-permute-start | bytes 1572872 | tf_op jit(solution)/shard_map/ppermute | solution.py:236
  24.3 3.1 %collective-permute-start.4 = (bf16[128,2048]{1,0:T(8,128)(2,1)S(1)}, bf16[128,2048]{1,0:T(8,128)(2,1)S(1)}, u32[]{:S(2)}, u32[]{:S(2)}) collective-permute-start(bf16[128,2048]{1,0:T(8,128)(2,1)S(1)} %get-tuple-element.16.a_ref), channel_id=1, source_target_pairs={{0,4},{4,0},{8,12},{12,8},{16,20},{20,16},{24,28},{28,24},{32,36},... | collective-permute-start | bytes 1572872 | tf_op jit(solution)/shard_map/ppermute | solution.py:233
  27.4 8.2 %collective-permute-done.5.c_ref = bf16[128,2048]{1,0:T(8,128)(2,1)S(1)} collective-permute-done((bf16[128,2048]{1,0:T(8,128)(2,1)S(1)}, bf16[128,2048]{1,0:T(8,128)(2,1)S(1)}, u32[]{:S(2)}, u32[]{:S(2)}) %collective-permute-start.5) | collective-permute-done | bytes 524320 | tf_op jit(solution)/shard_map/ppermute | solution.py:236
  35.6 3.7 %collective-permute-start.6 = (bf16[128,2048]{1,0:T(8,128)(2,1)S(1)}, bf16[128,2048]{1,0:T(8,128)(2,1)S(1)}, u32[]{:S(2)}, u32[]{:S(2)}) collective-permute-start(bf16[128,2048]{1,0:T(8,128)(2,1)S(1)} %collective-permute-done.5.c_ref), channel_id=1, source_target_pairs={{0,4},{4,0},{8,12},{12,8},{16,20},{20,16},{24,28},{28,24},{32,36},... | collective-permute-start | bytes 1572872 | tf_op jit(solution)/shard_map/ppermute | solution.py:233
  39.3 1.9 %collective-permute-start = (s32[4,128]{1,0:T(4,128)S(1)}, s32[4,128]{1,0:T(4,128)S(1)}, u32[]{:S(2)}, u32[]{:S(2)}) collective-permute-start(s32[4,128]{1,0:T(4,128)S(1)} %bitcast.14), channel_id=1, source_target_pairs={{0,4},{4,0},{8,12},{12,8},{16,20},{20,16},{24,28},{28,24},{32,36},... | collective-permute-start | bytes 6152 | tf_op jit(solution)/shard_map/ppermute | solution.py:233
  41.2 1.1 collective-permute-done.other_ids
  43.4 0.7 copy-done.2
  44.0 7.9 %all-to-all-done.w_ref.same_ref = bf16[128,32,128]{2,1,0:T(8,128)(2,1)S(1)} async-done(((bf16[128,32,128]{2,1,0:T(8,128)(2,1)}), bf16[128,32,128]{2,1,0:T(8,128)(2,1)S(1)}, u32[]{:S(2)}, u32[]{:S(2)}) %all-to-all-start) | async-done | bytes 1048608 | tf_op jit(solution)/shard_map/all_to_all | solution.py:239
  51.9 0.7 shard_map.97
  52.6 3.1 %collective-permute-start.7 = (bf16[256,256]{1,0:T(8,128)(2,1)S(1)}, bf16[256,256]{1,0:T(8,128)(2,1)S(1)}, u32[]{:S(2)}, u32[]{:S(2)}) collective-permute-start(bf16[256,256]{1,0:T(8,128)(2,1)S(1)} %get-tuple-element.18), channel_id=1, source_target_pairs={{0,1},{1,0},{2,3},{3,2},{4,5},{5,4},{6,7},{7,6},{8,9},{9,8},{10,11... | collective-permute-start | bytes 393224 | tf_op jit(solution)/shard_map/ppermute | solution.py:236
  55.8 3.6 %collective-permute-done.7.swapped_ref = bf16[256,256]{1,0:T(8,128)(2,1)S(1)} collective-permute-done((bf16[256,256]{1,0:T(8,128)(2,1)S(1)}, bf16[256,256]{1,0:T(8,128)(2,1)S(1)}, u32[]{:S(2)}, u32[]{:S(2)}) %collective-permute-start.7) | collective-permute-done | bytes 131104 | tf_op jit(solution)/shard_map/ppermute | solution.py:236
  59.4 1.0 shard_map.98
  60.3 48.3 %all_to_all.15 = bf16[128,48,128]{2,1,0:T(8,128)(2,1)S(1)} all-to-all(bf16[128,48,128]{2,1,0:T(8,128)(2,1)S(1)} %bitcast.10), channel_id=1, replica_groups=mesh['ep'=128,'dp'=4] {'ep'}, dimensions={0} | all-to-all | bytes 3145728 | tf_op jit(solution)/shard_map/all_to_all | solution.py:239
  108.6 8.2 %shard_map.99 = bf16[6144,128]{1,0:T(8,128)(2,1)} custom-call(bf16[6144,128]{1,0:T(8,128)(2,1)S(1)} %bitcast.11, bf16[512,1408]{1,0:T(8,128)(2,1)S(1)} %bitcast.12, bf16[1408,512]{1,0:T(8,128)(2,1)S(1)} %bitcast.13), custom_call_target="tpu_custom_call" | custom-call | flops 4429185024 | bytes 8388608 | tf_op jit(solution)/shard_map/pallas_call | solution.py:304
  116.9 8.1 %all-to-all-start.2 = ((bf16[128,48,128]{2,1,0:T(8,128)(2,1)}), bf16[128,48,128]{2,1,0:T(8,128)(2,1)}, u32[]{:S(2)}, u32[]{:S(2)}) async-start(bf16[128,48,128]{2,1,0:T(8,128)(2,1)} %bitcast.8), calls=%async_computation.2 | async-start | bytes 3145728 | tf_op jit(solution)/shard_map/all_to_all | solution.py:239
  125.0 3.1 %collective-permute-start.2 = (bf16[128,32,128]{2,1,0:T(8,128)(2,1)S(1)}, bf16[128,32,128]{2,1,0:T(8,128)(2,1)S(1)}, u32[]{:S(2)}, u32[]{:S(2)}) collective-permute-start(bf16[128,32,128]{2,1,0:T(8,128)(2,1)S(1)} %all-to-all-done.w_ref.same_ref), channel_id=1, source_target_pairs={{0,1},{1,0},{2,3},{3,2},{4,5},{5,4},{6,7},{7,6},{8,9},{9,8},{10,11... | collective-permute-start | bytes 3145736 | tf_op jit(solution)/shard_map/ppermute | solution.py:236
  128.1 3.1 %collective-permute-start.1 = (bf16[128,32,128]{2,1,0:T(8,128)(2,1)S(1)}, bf16[128,32,128]{2,1,0:T(8,128)(2,1)S(1)}, u32[]{:S(2)}, u32[]{:S(2)}) collective-permute-start(bf16[128,32,128]{2,1,0:T(8,128)(2,1)S(1)} %all-to-all-done.w_ref.same_ref), channel_id=1, source_target_pairs={{0,4},{4,0},{8,12},{12,8},{16,20},{20,16},{24,28},{28,24},{32,36},... | collective-permute-start | bytes 3145736 | tf_op jit(solution)/shard_map/ppermute | solution.py:233
  131.3 19.4 %collective-permute-done.2.plane_ref = bf16[128,32,128]{2,1,0:T(8,128)(2,1)S(1)} collective-permute-done((bf16[128,32,128]{2,1,0:T(8,128)(2,1)S(1)}, bf16[128,32,128]{2,1,0:T(8,128)(2,1)S(1)}, u32[]{:S(2)}, u32[]{:S(2)}) %collective-permute-start.2) | collective-permute-done | bytes 1048608 | tf_op jit(solution)/shard_map/ppermute | solution.py:236
  150.7 3.7 %collective-permute-start.3 = (bf16[128,32,128]{2,1,0:T(8,128)(2,1)S(1)}, bf16[128,32,128]{2,1,0:T(8,128)(2,1)}, u32[]{:S(2)}, u32[]{:S(2)}) collective-permute-start(bf16[128,32,128]{2,1,0:T(8,128)(2,1)S(1)} %collective-permute-done.2.plane_ref), channel_id=1, source_target_pairs={{0,4},{4,0},{8,12},{12,8},{16,20},{20,16},{24,28},{28,24},{32,36},... | collective-permute-start | bytes 3145736 | tf_op jit(solution)/shard_map/ppermute | solution.py:233
  154.4 2.4 %collective-permute-done.3.far_ref = bf16[128,32,128]{2,1,0:T(8,128)(2,1)} collective-permute-done((bf16[128,32,128]{2,1,0:T(8,128)(2,1)S(1)}, bf16[128,32,128]{2,1,0:T(8,128)(2,1)}, u32[]{:S(2)}, u32[]{:S(2)}) %collective-permute-start.3) | collective-permute-done | bytes 1048608 | tf_op jit(solution)/shard_map/ppermute | solution.py:233
  156.7 9.2 %all-to-all-done.2 = bf16[128,48,128]{2,1,0:T(8,128)(2,1)} async-done(((bf16[128,48,128]{2,1,0:T(8,128)(2,1)}), bf16[128,48,128]{2,1,0:T(8,128)(2,1)}, u32[]{:S(2)}, u32[]{:S(2)}) %all-to-all-start.2) | async-done | bytes 1572896 | tf_op jit(solution)/shard_map/all_to_all | solution.py:239
  165.9 7.1 %shard_map.100 = (bf16[128,2048]{1,0:T(8,128)(2,1)}, bf16[128,2048]{1,0:T(8,128)(2,1)}) custom-call(bf16[128,768]{1,0:T(8,128)(2,1)S(1)} %copy-done.1, bf16[128,768]{1,0:T(8,128)(2,1)S(1)} %copy-done.3, bf16[128,32,128]{2,1,0:T(8,128)(2,1)S(1)} %all-to-all-done.w_ref.same_ref, bf16[128,32,128]{2,1,0:T(8,128)(2,1)S(1)} %collective-permute-done.1.next_ref, ...), custom_call_target="tpu_custom_call" | custom-call | flops 536870912 | bytes 7340032 | tf_op jit(solution)/shard_map/pallas_call | solution.py:324
  (26 shorter events, 1.1 us)
Async XLA Ops:
  0.6 20.4 %copy-start.9 = (bf16[128,2048]{1,0:T(8,128)(2,1)S(1)}, bf16[128,2048]{1,0:T(8,128)(2,1)}, u32[]{:S(2)}) copy-start(bf16[128,2048]{1,0:T(8,128)(2,1)} %param.15) | copy-start | bytes 1572868
  0.6 20.4 %copy-start.10 = (bf16[128,2048]{1,0:T(8,128)(2,1)S(1)}, bf16[128,2048]{1,0:T(8,128)(2,1)}, u32[]{:S(2)}) copy-start(bf16[128,2048]{1,0:T(8,128)(2,1)} %param.8) | copy-start | bytes 1572868
  2.6 49.3 %all-to-all-start = ((bf16[128,32,128]{2,1,0:T(8,128)(2,1)}), bf16[128,32,128]{2,1,0:T(8,128)(2,1)S(1)}, u32[]{:S(2)}, u32[]{:S(2)}) async-start(bf16[128,32,128]{2,1,0:T(8,128)(2,1)} %bitcast.17), calls=%async_computation | async-start | bytes 2097152 | tf_op jit(solution)/shard_map/all_to_all | solution.py:239
  21.0 18.3 %copy-start.6 = (s32[128,4]{0,1:T(4,128)S(1)}, s32[128,4]{0,1:T(4,128)}, u32[]{:S(2)}) copy-start(s32[128,4]{0,1:T(4,128)} %param.9) | copy-start | bytes 6148
  21.0 21.3 %copy-start.7 = (f32[128,4]{0,1:T(4,128)S(1)}, f32[128,4]{0,1:T(4,128)}, u32[]{:S(2)}) copy-start(f32[128,4]{0,1:T(4,128)} %param.10) | copy-start | bytes 6148
  21.1 14.4 %collective-permute-start.5 = (bf16[128,2048]{1,0:T(8,128)(2,1)S(1)}, bf16[128,2048]{1,0:T(8,128)(2,1)S(1)}, u32[]{:S(2)}, u32[]{:S(2)}) collective-permute-start(bf16[128,2048]{1,0:T(8,128)(2,1)S(1)} %get-tuple-element.20), channel_id=1, source_target_pairs={{0,1},{1,0},{2,3},{3,2},{4,5},{5,4},{6,7},{7,6},{8,9},{9,8},{10,11... | collective-permute-start | bytes 1572872 | tf_op jit(solution)/shard_map/ppermute | solution.py:236
  24.3 19.8 %collective-permute-start.4 = (bf16[128,2048]{1,0:T(8,128)(2,1)S(1)}, bf16[128,2048]{1,0:T(8,128)(2,1)S(1)}, u32[]{:S(2)}, u32[]{:S(2)}) collective-permute-start(bf16[128,2048]{1,0:T(8,128)(2,1)S(1)} %get-tuple-element.16.a_ref), channel_id=1, source_target_pairs={{0,4},{4,0},{8,12},{12,8},{16,20},{20,16},{24,28},{28,24},{32,36},... | collective-permute-start | bytes 1572872 | tf_op jit(solution)/shard_map/ppermute | solution.py:233
  35.6 8.5 %collective-permute-start.6 = (bf16[128,2048]{1,0:T(8,128)(2,1)S(1)}, bf16[128,2048]{1,0:T(8,128)(2,1)S(1)}, u32[]{:S(2)}, u32[]{:S(2)}) collective-permute-start(bf16[128,2048]{1,0:T(8,128)(2,1)S(1)} %collective-permute-done.5.c_ref), channel_id=1, source_target_pairs={{0,4},{4,0},{8,12},{12,8},{16,20},{20,16},{24,28},{28,24},{32,36},... | collective-permute-start | bytes 1572872 | tf_op jit(solution)/shard_map/ppermute | solution.py:233
  39.3 3.1 %collective-permute-start = (s32[4,128]{1,0:T(4,128)S(1)}, s32[4,128]{1,0:T(4,128)S(1)}, u32[]{:S(2)}, u32[]{:S(2)}) collective-permute-start(s32[4,128]{1,0:T(4,128)S(1)} %bitcast.14), channel_id=1, source_target_pairs={{0,4},{4,0},{8,12},{12,8},{16,20},{20,16},{24,28},{28,24},{32,36},... | collective-permute-start | bytes 6152 | tf_op jit(solution)/shard_map/ppermute | solution.py:233
  42.7 0.7 copy-start
  43.3 0.7 copy-start.2
  52.6 6.7 %collective-permute-start.7 = (bf16[256,256]{1,0:T(8,128)(2,1)S(1)}, bf16[256,256]{1,0:T(8,128)(2,1)S(1)}, u32[]{:S(2)}, u32[]{:S(2)}) collective-permute-start(bf16[256,256]{1,0:T(8,128)(2,1)S(1)} %get-tuple-element.18), channel_id=1, source_target_pairs={{0,1},{1,0},{2,3},{3,2},{4,5},{5,4},{6,7},{7,6},{8,9},{9,8},{10,11... | collective-permute-start | bytes 393224 | tf_op jit(solution)/shard_map/ppermute | solution.py:236
  60.3 48.3 %copy-start.4 = (bf16[1,512,1408]{2,1,0:T(8,128)(2,1)S(1)}, bf16[1,512,1408]{2,1,0:T(8,128)(2,1)}, u32[]{:S(2)}) copy-start(bf16[1,512,1408]{2,1,0:T(8,128)(2,1)} %param.13) | copy-start | bytes 4325380
  60.3 48.3 %copy-start.5 = (bf16[1,1408,512]{2,1,0:T(8,128)(2,1)S(1)}, bf16[1,1408,512]{2,1,0:T(8,128)(2,1)}, u32[]{:S(2)}) copy-start(bf16[1,1408,512]{2,1,0:T(8,128)(2,1)} %param.14) | copy-start | bytes 4325380
  116.9 49.0 %copy-start.1 = (bf16[128,768]{1,0:T(8,128)(2,1)S(1)}, bf16[128,768]{1,0:T(8,128)(2,1)}, u32[]{:S(2)}) copy-start(bf16[128,768]{1,0:T(8,128)(2,1)} %copy-done) | copy-start | bytes 589828
  116.9 49.0 %copy-start.3 = (bf16[128,768]{1,0:T(8,128)(2,1)S(1)}, bf16[128,768]{1,0:T(8,128)(2,1)}, u32[]{:S(2)}) copy-start(bf16[128,768]{1,0:T(8,128)(2,1)} %copy-done.2) | copy-start | bytes 589828
  116.9 49.0 %all-to-all-start.2 = ((bf16[128,48,128]{2,1,0:T(8,128)(2,1)}), bf16[128,48,128]{2,1,0:T(8,128)(2,1)}, u32[]{:S(2)}, u32[]{:S(2)}) async-start(bf16[128,48,128]{2,1,0:T(8,128)(2,1)} %bitcast.8), calls=%async_computation.2 | async-start | bytes 3145728 | tf_op jit(solution)/shard_map/all_to_all | solution.py:239
  125.0 25.7 %collective-permute-start.2 = (bf16[128,32,128]{2,1,0:T(8,128)(2,1)S(1)}, bf16[128,32,128]{2,1,0:T(8,128)(2,1)S(1)}, u32[]{:S(2)}, u32[]{:S(2)}) collective-permute-start(bf16[128,32,128]{2,1,0:T(8,128)(2,1)S(1)} %all-to-all-done.w_ref.same_ref), channel_id=1, source_target_pairs={{0,1},{1,0},{2,3},{3,2},{4,5},{5,4},{6,7},{7,6},{8,9},{9,8},{10,11... | collective-permute-start | bytes 3145736 | tf_op jit(solution)/shard_map/ppermute | solution.py:236
  128.1 26.2 %collective-permute-start.1 = (bf16[128,32,128]{2,1,0:T(8,128)(2,1)S(1)}, bf16[128,32,128]{2,1,0:T(8,128)(2,1)S(1)}, u32[]{:S(2)}, u32[]{:S(2)}) collective-permute-start(bf16[128,32,128]{2,1,0:T(8,128)(2,1)S(1)} %all-to-all-done.w_ref.same_ref), channel_id=1, source_target_pairs={{0,4},{4,0},{8,12},{12,8},{16,20},{20,16},{24,28},{28,24},{32,36},... | collective-permute-start | bytes 3145736 | tf_op jit(solution)/shard_map/ppermute | solution.py:233
  150.7 15.2 %copy-start.8 = (bf16[128,32,128]{2,1,0:T(8,128)(2,1)}, bf16[128,32,128]{2,1,0:T(8,128)(2,1)S(1)}, u32[]{:S(2)}) copy-start(bf16[128,32,128]{2,1,0:T(8,128)(2,1)S(1)} %collective-permute-done.2.plane_ref) | copy-start | bytes 3145732
  150.7 6.1 %collective-permute-start.3 = (bf16[128,32,128]{2,1,0:T(8,128)(2,1)S(1)}, bf16[128,32,128]{2,1,0:T(8,128)(2,1)}, u32[]{:S(2)}, u32[]{:S(2)}) collective-permute-start(bf16[128,32,128]{2,1,0:T(8,128)(2,1)S(1)} %collective-permute-done.2.plane_ref), channel_id=1, source_target_pairs={{0,4},{4,0},{8,12},{12,8},{16,20},{20,16},{24,28},{28,24},{32,36},... | collective-permute-start | bytes 3145736 | tf_op jit(solution)/shard_map/ppermute | solution.py:233
